TPU v7x, 256 devices: a whole 4x4x8 slice. The times are simulated.
256 devices in a mesh: dp: 32 (over z_hi, x, y), tensor: 8 (over z_lo, core).
Axes of the slice: x: 4, y: 4, z: 8 (z_hi: 2, z_lo: 4; z = z_hi * 4 + z_lo), core: 2. Of those that a mesh axis runs over, the one named last changes fastest.
Arguments:
- hidden_rows: bfloat16 [512, 2, 8192], P('dp', None, 'tensor'), may hold values from -6 to 6
- key_value_weight: bfloat16 [8192, 2048], P(None, 'tensor'), may hold values from -0.0625 to 0.0625
- adapter_down_weight: bfloat16 [128, 8192, 128], P('dp', 'tensor'), may hold values from -0.0625 to 0.0625
- adapter_up_weight: bfloat16 [128, 64, 2048], P('dp', None, 'tensor'), may hold values from -0.75 to 0.75
- adapter_ids: int32 [512], replicated, may hold values from 0 to 127
- kv_lengths: int32 [512], P('dp'), may hold values from 2 to 512, as said below
- queries: bfloat16 [512, 2, 8192], P('dp', None, 'tensor'), may hold values from -120 to 120
- k_cache: bfloat16 [512, 512, 1024], P('dp', None, 'tensor'), may hold values from -6 to 6
- value_cache: bfloat16 [512, 512, 1024], P('dp', None, 'tensor'), may hold values from -6 to 6
Outputs:
- new_kv: bfloat16 [512, 2, 2048], P('dp', None, 'tensor')
- attended: bfloat16 [512, 2, 8192], P('dp', None, 'tensor')
Inputs may be any that keep to these rules, and one draw needn't show every extreme that they name: `kv_lengths`: at least one row has exactly 512 positions in use.
All inputs are finite; a program needn't handle non-finite values.
Results may differ from a plain program's by a relative error of at most 0.0057.
Values may be sent and summed in bfloat16 or wider, within the bound.
No kernel may reach another device: no remote copies, remote signals or barrier semaphores. Data moves between devices by JAX's collectives and lax.ppermute only.
A program may use at most 128 MiB of HBM per device.

v0:
```python
import math

import jax
import jax.numpy as jnp
from jax import lax
from jax.sharding import PartitionSpec as P

HEAD_SIZE = 128


def rotate(keys_in, positions):
    half_width = keys_in.shape[-1] // 2
    frequency = jnp.exp(
        jnp.arange(half_width, dtype=jnp.float32) * (-2.0 * math.log(500000.0) / keys_in.shape[-1])
    )
    angles = positions.astype(jnp.float32)[..., None, None] * frequency
    cosine = jnp.cos(angles)
    sine_part = jnp.sin(angles)
    lower_half = keys_in[..., :half_width]
    upper_half = keys_in[..., half_width:]
    return jnp.concatenate(
        [
            lower_half * cosine - upper_half * sine_part,
            upper_half * cosine + lower_half * sine_part,
        ],
        -1,
    )


def select_up(one_hot, up_tables):
    return jnp.einsum("ra,akc->rkc", one_hot, up_tables, preferred_element_type=jnp.float32).astype(
        jnp.bfloat16
    )


def apply_up_weight(adapter_down_rows, chosen_up_weight, adapter_rank_width):
    decode_row_count, decode_step_count = (adapter_down_rows.shape[0], adapter_down_rows.shape[1])
    up_split = chosen_up_weight.reshape(decode_row_count, adapter_rank_width, -1, 2, HEAD_SIZE)
    key_update = jnp.einsum(
        "rsk,rkhd->rshd",
        adapter_down_rows[..., :adapter_rank_width],
        up_split[:, :, :, 0],
        preferred_element_type=jnp.float32,
    )
    value_update = jnp.einsum(
        "rsk,rkhd->rshd",
        adapter_down_rows[..., adapter_rank_width:],
        up_split[:, :, :, 1],
        preferred_element_type=jnp.float32,
    )
    return jnp.stack([key_update, value_update], 3).reshape(decode_row_count, decode_step_count, -1)


def per_device(
    hidden_rows,
    key_value_weight,
    adapter_down_weight,
    adapter_up_weight,
    adapter_ids,
    kv_lengths,
    queries,
    k_cache,
    value_cache,
):
    rows_per_device, decode_step_count = (hidden_rows.shape[0], hidden_rows.shape[1])
    owned_count = adapter_down_weight.shape[0]
    adapter_rank_width = adapter_down_weight.shape[2] // 2
    key_value_heads = key_value_weight.shape[1] // (2 * HEAD_SIZE)
    first_owned = lax.axis_index("dp") * owned_count
    owner_hot = (
        adapter_ids[:, None] == first_owned + jnp.arange(owned_count, dtype=jnp.int32)[None, :]
    ).astype(jnp.float32)
    base_projection = jnp.einsum(
        "rsd,dc->rsc",
        lax.all_gather(hidden_rows, "tensor", axis=2, tiled=True),
        key_value_weight,
        preferred_element_type=jnp.float32,
    )
    products = jnp.einsum(
        "rsd,adk->rsak",
        lax.all_gather(hidden_rows, "dp", axis=0, tiled=True),
        adapter_down_weight,
        preferred_element_type=jnp.float32,
    )
    partial_down = jnp.sum(products * owner_hot[:, None, :, None], axis=2)
    down_all = lax.psum(partial_down, "tensor").astype(jnp.bfloat16)
    hot_local = owner_hot.astype(jnp.bfloat16)
    adapter_update = lax.psum_scatter(
        apply_up_weight(down_all, select_up(hot_local, adapter_up_weight), adapter_rank_width),
        "dp",
        scatter_dimension=0,
        tiled=True,
    )
    projected_rows = (base_projection + adapter_update).reshape(
        rows_per_device, decode_step_count, key_value_heads, 2, HEAD_SIZE
    )
    positions = kv_lengths[:, None] + jnp.arange(decode_step_count, dtype=jnp.int32)[None, :]
    keys_new = rotate(projected_rows[:, :, :, 0], positions)
    fresh_key_value = jnp.stack([keys_new, projected_rows[:, :, :, 1]], 3).astype(jnp.bfloat16)
    new_kv = fresh_key_value.reshape(
        rows_per_device, decode_step_count, key_value_heads * 2 * HEAD_SIZE
    )
    context = k_cache.shape[1]
    query_group_size = queries.shape[2] // (key_value_heads * HEAD_SIZE)
    score_scale = 1.0 / math.sqrt(HEAD_SIZE)
    query_head_count = queries.reshape(
        rows_per_device, decode_step_count, key_value_heads, query_group_size, HEAD_SIZE
    )
    stored_keys = k_cache.reshape(rows_per_device, context, key_value_heads, HEAD_SIZE)
    stored_values = value_cache.reshape(rows_per_device, context, key_value_heads, HEAD_SIZE)
    old_scores = (
        jnp.einsum(
            "rshgd,rjhd->rshgj", query_head_count, stored_keys, preferred_element_type=jnp.float32
        )
        * score_scale
    )
    valid_mask = jnp.arange(context, dtype=jnp.int32)[None, :] < kv_lengths[:, None]
    old_scores = jnp.where(valid_mask[:, None, None, None, :], old_scores, -jnp.inf)
    new_scores = (
        jnp.einsum(
            "rshgd,rthd->rshgt",
            query_head_count,
            fresh_key_value[:, :, :, 0],
            preferred_element_type=jnp.float32,
        )
        * score_scale
    )
    causal_mask = jnp.arange(decode_step_count)[None, :] <= jnp.arange(decode_step_count)[:, None]
    new_scores = jnp.where(causal_mask[None, :, None, None, :], new_scores, -jnp.inf)
    scores = jnp.concatenate([old_scores, new_scores], -1)
    row_max = jnp.max(scores, -1, keepdims=True)
    exponent = jnp.exp(scores - row_max)
    weights = (exponent / jnp.sum(exponent, -1, keepdims=True)).astype(jnp.bfloat16)
    attention_output = jnp.einsum(
        "rshgj,rjhd->rshgd",
        weights[..., :context],
        stored_values,
        preferred_element_type=jnp.float32,
    )
    attention_output = attention_output + jnp.einsum(
        "rshgt,rthd->rshgd",
        weights[..., context:],
        fresh_key_value[:, :, :, 1],
        preferred_element_type=jnp.float32,
    )
    attended = attention_output.astype(jnp.bfloat16).reshape(
        rows_per_device, decode_step_count, key_value_heads * query_group_size * HEAD_SIZE
    )
    return (new_kv, attended)


def solution(mesh):
    return jax.shard_map(
        per_device,
        mesh=mesh,
        in_specs=(
            P("dp", None, "tensor"),
            P(None, "tensor"),
            P("dp", "tensor", None),
            P("dp", None, "tensor"),
            P(),
            P("dp"),
            P("dp", None, "tensor"),
            P("dp", None, "tensor"),
            P("dp", None, "tensor"),
        ),
        out_specs=(P("dp", None, "tensor"), P("dp", None, "tensor")),
        check_vma=False,
    )
```

profile of v0, /device:TPU:32, one launch (start us, length us, event | category | flops | bytes accessed | tf_op | source)
XLA Modules:
  0.0 391.8 jit_solution(3631806539239943682)
XLA Ops:
  7.2 1.6 copy.64
  8.9 11.2 %convolution_convert_fusion = bf16[512,64,256]{0,2,1:T(8,128)(2,1)} fusion(bf16[4,64,256]{2,1,0:T(8,128)(2,1)} %param.12, s32[512]{0:T(512)} %param.13, s32[4]{0:T(128)S(1)} %iota_add_fusion), kind=kOutput, calls=%fused_computation | convolution fusion | flops 75503616 | bytes 16910352 | tf_op jit(solution)/shard_map/ra,akc->rkc/dot_general | solution.py:31
  20.1 11.6 %fusion.66 = (bf16[512,64,1,1,128]{0,4,3,1,2:T(8,128)(2,1)}, bf16[512,64,1,1,128]{0,4,3,1,2:T(8,128)(2,1)}) fusion(bf16[512,64,1,2,128]{0,4,3,1,2:T(8,128)(2,1)} %bitcast.120), kind=kLoop, calls=%fused_computation.62 | loop fusion | bytes 33554432 | tf_op jit(solution)/shard_map/slice | solution.py:42
  31.7 12.1 %copy.93 = bf16[512,64,1,1,128]{4,1,0,3,2:T(8,128)(2,1)} copy(bf16[512,64,1,1,128]{0,4,3,1,2:T(8,128)(2,1)} %get-tuple-element.11) | data formatting | bytes 16777216
  43.8 12.2 %copy.92 = bf16[512,64,1,1,128]{4,1,0,3,2:T(8,128)(2,1)} copy(bf16[512,64,1,1,128]{0,4,3,1,2:T(8,128)(2,1)} %get-tuple-element.10) | data formatting | bytes 16777216
  56.0 49.7 %all-gather.2.cloned.1.call-done = bf16[512,2,1024]{2,0,1:T(8,128)(2,1)} async-done(((bf16[16,2,1024]{2,0,1:T(8,128)(2,1)}), bf16[512,2,1024]{2,0,1:T(8,128)(2,1)}) %all-gather.2.cloned.1.call-update) | async-done | bytes 2097168 | tf_op jit(solution)/shard_map/all_gather | solution.py:81
  105.7 2.9 multiply_reduce_fusion
  108.6 0.4 copy.66
  109.0 30.1 %all-reduce.1 = bf16[512,2,128]{2,1,0:T(2,128)(2,1)S(1)} all-reduce(f32[512,2,128]{2,1,0:T(2,128)S(1)} %copy.66), channel_id=1, replica_groups=mesh['dp'=32,'tensor'=8] {'tensor'}, use_global_device_ids=true, to_apply=%region_1.0 | all-reduce | flops 131072 | bytes 786432 | tf_op jit(solution)/shard_map/psum | solution.py:86
  139.2 5.7 %fusion.23 = f32[512,2,1,1,128]{4,1,0,3,2:T(2,128)S(1)} fusion(bf16[512,64,1,1,128]{4,1,0,3,2:T(8,128)(2,1)} %copy.93, bf16[512,2,128]{2,1,0:T(2,128)(2,1)S(1)} %all-reduce.1), kind=kOutput, calls=%fused_computation.17 | convolution fusion | flops 16777216 | bytes 9175040 | tf_op jit(solution)/shard_map/rsk,rkhd->rshd/dot_general | solution.py:45
  144.9 5.7 %fusion.20 = f32[512,2,1,1,128]{4,1,0,3,2:T(2,128)S(1)} fusion(bf16[512,64,1,1,128]{4,1,0,3,2:T(8,128)(2,1)} %copy.92, bf16[512,2,128]{2,1,0:T(2,128)(2,1)S(1)} %all-reduce.1), kind=kOutput, calls=%fused_computation.16 | convolution fusion | flops 16777216 | bytes 9175040 | tf_op jit(solution)/shard_map/rsk,rkhd->rshd/dot_general | solution.py:39
  150.5 0.5 pad_maximum_fusion
  151.0 0.8 copy.70
  151.8 1.8 reshape.286
  153.9 16.6 %all_gather.6 = bf16[16,2,8192]{2,0,1:T(8,128)(2,1)S(1)} all-gather(bf16[16,2,1024]{2,0,1:T(8,128)(2,1)S(1)} %copy-done.1), channel_id=1, replica_groups=mesh['dp'=32,'tensor'=8] {'tensor'}, dimensions={2}, use_global_device_ids=true | all-gather | bytes 589824 | tf_op jit(solution)/shard_map/all_gather | solution.py:75
  170.5 0.8 fusion.68
  171.2 206.2 %reduce-scatter.2.cloned.1.call-done = f32[16,2,256]{2,0,1:T(8,128)} async-done(((f32[512,2,256]{2,0,1:T(8,128)}), f32[16,2,256]{2,0,1:T(8,128)}) %reduce-scatter.2.cloned.1.call-update) | async-done | bytes 32784 | tf_op jit(solution)/shard_map/reduce_scatter | solution.py:88
  377.4 3.0 fusion.46
  380.8 0.6 reshape.302
  381.4 0.2 fusion.69
  381.7 0.3 fusion.51
  381.9 0.2 divide_convert_fusion
  382.3 2.0 fusion.43
  384.3 0.7 reshape.293
  (32 shorter events, 0.8 us)
Async XLA Ops:
  7.2 163.3 %copy-start = (bf16[16,512,128]{2,1,0:T(8,128)(2,1)S(1)}, bf16[16,512,128]{2,1,0:T(8,128)(2,1)}, u32[]{:S(2)}) copy-start(bf16[16,512,128]{2,1,0:T(8,128)(2,1)} %param.16) | copy-start | bytes 6291460
  7.2 98.5 %all-gather.2.cloned.1.call-start = ((), (), s32[]{:S(2)}) async-start(), calls=%async_computation.1 | async-start | bytes 2162688 | tf_op jit(solution)/shard_map/all_gather | solution.py:81
  8.9 368.5 %reduce-scatter.2.cloned.1.call-start = ((), (), s32[]{:S(2)}) async-start(), calls=%async_computation.2 | async-start | bytes 1081344 | tf_op jit(solution)/shard_map/reduce_scatter | solution.py:88
  43.8 12.2 %copy-start.3 = (s32[512]{0:T(512)S(1)}, s32[512]{0:T(512)}, u32[]{:S(2)}) copy-start(s32[512]{0:T(512)} %param.13) | copy-start | bytes 6148
  43.8 61.9 %copy-start.5 = (bf16[4,1024,128]{2,1,0:T(8,128)(2,1)S(1)}, bf16[4,1024,128]{2,1,0:T(8,128)(2,1)}, u32[]{:S(2)}) copy-start(bf16[4,1024,128]{2,1,0:T(8,128)(2,1)} %param.11) | copy-start | bytes 3145732
  150.5 3.1 copy-start.2
  150.5 3.2 copy-start.4
  150.5 3.3 copy-start.1
Sparse Core Ops, SparseCore 0:
  12.1 93.5 all-gather.1
  153.8 223.5 reduce-scatter.1
where the time goes:
time: 393 us; the launch traced here: 392 us
  waiting for transfers between devices  256 us (65%)
  blocking collectives  46.7 us (12%)
  local copies, waits for them, and re-layouts  41.9 us (11%)
  matrix products  31.6 us (8%)
  between operations  14.2 us (4%)
    reduce_scatter x1, waiting for transfers between devices, per_device(): lax.psum_scatter(apply_up_weight(down_all, select_up(hot_local, adapter_u...  206 us
    all_gather x1, waiting for transfers between devices, per_device(): lax.all_gather(hidden_rows, 'dp', axis=0, tiled=True)  49.7 us
    psum x1, blocking collectives, per_device(): down_all = lax.psum(partial_down, 'tensor').astype(jnp.bfloat16)  30.1 us
    unnamed x17, local copies, waits for them, and re-layouts  26.5 us
    all_gather x1, blocking collectives, per_device(): lax.all_gather(hidden_rows, 'tensor', axis=2, tiled=True)  16.6 us
    slice x1, local copies, waits for them, and re-layouts, apply_up_weight(): up_split[:, :, :, 0]  11.6 us
    dot_general x1, matrix products, select_up(): jnp.einsum('ra,akc->rkc', one_hot, up_tables, preferred_element_type=jnp....  11.2 us
  transfers between devices with their start and end apart: 2, of which 2 were waited for; matrix products, arithmetic and copies ran while one was open for 12% of the time, Pallas kernels for 0%

commit v1 on v0

v1 whole, which is shorter than its diff:
```python
import math

import jax
import jax.numpy as jnp
from jax import lax
from jax.sharding import PartitionSpec as P

HEAD_SIZE = 128
F32 = jnp.float32
BF16 = jnp.bfloat16
BOTH = ("dp", "tensor")


def pairs_of(move):
    pairs = []
    for d in range(32):
        for j in range(8):
            z, x, y, t, c = d // 16, d // 4 % 4, d % 4, j // 2, j % 2
            z, x, y, t, c = move(z, x, y, t, c)
            pairs.append((d * 8 + j, (z * 16 + x * 4 + y) * 8 + t * 2 + c))
    return pairs


def swap_core(value):
    return lax.ppermute(value, BOTH, pairs_of(lambda z, x, y, t, c: (z, x, y, t, c ^ 1)))


def cross_z(value):
    return lax.ppermute(value, BOTH, pairs_of(lambda z, x, y, t, c: (z ^ c, x, y, t, c)))


def first_axis(value, k):
    return lax.ppermute(
        value,
        BOTH,
        pairs_of(lambda z, x, y, t, c: (z, x ^ (0 if c else k), y ^ (k if c else 0), t, c)),
    )


def second_axis(value, k):
    return lax.ppermute(
        value,
        BOTH,
        pairs_of(lambda z, x, y, t, c: (z, x ^ (k if c else 0), y ^ (0 if c else k), t, c)),
    )


def along_z(value, k):
    return lax.ppermute(value, BOTH, pairs_of(lambda z, x, y, t, c: (z, x, y, t ^ k, c)))


def cached_attention(queries, k_cache, value_cache, kv_lengths):
    rows, context = k_cache.shape[0], k_cache.shape[1]
    scores = jnp.einsum("rqd,rjd->rqj", queries, k_cache, preferred_element_type=F32)
    scores = scores * (1.0 / math.sqrt(HEAD_SIZE))
    valid = jnp.arange(context, dtype=jnp.int32)[None, :] < kv_lengths[:, None]
    scores = jnp.where(valid[:, None, :], scores, -jnp.inf)
    top = jnp.max(scores, -1, keepdims=True)
    weight = jnp.exp(scores - top)
    total = jnp.sum(weight, -1, keepdims=True)
    gathered = jnp.einsum(
        "rqj,rjd->rqd", weight.astype(BF16), value_cache, preferred_element_type=F32
    )
    return top, total, gathered


def per_device(
    hidden_rows,
    key_value_weight,
    adapter_down_weight,
    adapter_up_weight,
    adapter_ids,
    kv_lengths,
    queries,
    k_cache,
    value_cache,
):
    rows, steps, width = hidden_rows.shape
    owned = adapter_down_weight.shape[0]
    rank = adapter_down_weight.shape[2] // 2
    group = rows * steps
    me = lax.axis_index("dp")
    j = lax.axis_index("tensor")
    t, c = j // 2, j % 2

    own = hidden_rows.reshape(group, width)
    pair = jnp.concatenate([own, swap_core(own)], 1)
    down_weight = jnp.concatenate([adapter_down_weight, swap_core(adapter_down_weight)], 1)
    up_other = swap_core(adapter_up_weight)

    start = cross_z(pair)
    line = jnp.concatenate([start] + [first_axis(start, k) for k in (1, 2, 3)], 0)
    blocks = {0: line}
    for k in (1, 3, 2):
        blocks[k] = second_axis(line, k)

    k2 = jnp.arange(4, dtype=jnp.int32)[:, None]
    k1 = jnp.arange(4, dtype=jnp.int32)[None, :]
    groups = me ^ (16 * c) ^ jnp.where(c == 0, 4 * k1 + k2, 4 * k2 + k1)
    ids = adapter_ids.reshape(32, rows)[groups]
    hot = ids[..., None] == me * owned + jnp.arange(owned, dtype=jnp.int32)
    hot = jnp.repeat(hot, steps, axis=2).reshape(4, 4 * group, owned)

    partial = []
    for k in range(4):
        products = jnp.einsum("rd,adk->rak", blocks[k], down_weight, preferred_element_type=F32)
        partial.append(jnp.sum(jnp.where(hot[k][:, :, None], products, 0.0), axis=1))
    partial = jnp.stack(partial)

    mine = lax.dynamic_index_in_dim(partial, t, 0, keepdims=False)
    rounded = partial.astype(BF16)
    for m in (1, 2, 3):
        sent = lax.dynamic_index_in_dim(rounded, t ^ m, 0, keepdims=False)
        mine = mine + along_z(sent, m).astype(F32)
    mine = mine.astype(BF16)
    low = jnp.stack([mine] + [along_z(mine, m) for m in (1, 2, 3)])

    hot_slots = jnp.stack([lax.dynamic_index_in_dim(hot, t ^ m, 0, keepdims=False) for m in range(4)])
    spread = jnp.where(hot_slots[..., None], low[:, :, None, :], 0.0).astype(BF16)
    spread_key = spread[..., :rank].reshape(-1, owned * rank)
    spread_value = spread[..., rank:].reshape(-1, owned * rank)

    def up_columns(first):
        columns = [
            u[:, :, first : first + HEAD_SIZE].reshape(owned * rank, HEAD_SIZE)
            for u in (adapter_up_weight, up_other)
        ]
        return jnp.concatenate(columns, 1)

    delta_key = jnp.dot(spread_key, up_columns(0), preferred_element_type=F32).astype(BF16)
    delta_value = jnp.dot(spread_value, up_columns(HEAD_SIZE), preferred_element_type=F32).astype(
        BF16
    )
    delta = jnp.concatenate(
        [
            delta_key[:, :HEAD_SIZE],
            delta_value[:, :HEAD_SIZE],
            delta_key[:, HEAD_SIZE:],
            delta_value[:, HEAD_SIZE:],
        ],
        1,
    ).reshape(4, 4 * group, 4 * HEAD_SIZE)

    back = lax.dynamic_index_in_dim(delta, t, 0, keepdims=False)
    for k in (1, 3, 2):
        back = back + second_axis(lax.dynamic_index_in_dim(delta, t ^ k, 0, keepdims=False), k)
    back = back.reshape(4, group, 4 * HEAD_SIZE)
    home = back[0]
    for k in (1, 3, 2):
        home = home + first_axis(back[k], k)
    home = cross_z(home)
    update = home[:, : 2 * HEAD_SIZE] + swap_core(home[:, 2 * HEAD_SIZE :])

    chips = [pair] + [along_z(pair, m) for m in (1, 2, 3)]
    full = jnp.zeros((4, 2, group, width), BF16)
    for m in range(4):
        both = jnp.stack([chips[m][:, :width], chips[m][:, width:]])
        both = jnp.where(c == 0, both, both[::-1])
        full = lax.dynamic_update_slice(full, both[None], (t ^ m, 0, 0, 0))
    full = full.transpose(2, 0, 1, 3).reshape(group, 8 * width)
    base = jnp.dot(full, key_value_weight, preferred_element_type=F32)

    projected = (base + update.astype(F32)).reshape(rows, steps, 2, HEAD_SIZE)
    half = HEAD_SIZE // 2
    frequency = jnp.exp(
        jnp.arange(half, dtype=F32) * (-2.0 * math.log(500000.0) / HEAD_SIZE)
    )
    positions = kv_lengths[:, None] + jnp.arange(steps, dtype=jnp.int32)[None, :]
    angles = positions.astype(F32)[..., None] * frequency
    cosine, sine = jnp.cos(angles), jnp.sin(angles)
    low_half, high_half = projected[:, :, 0, :half], projected[:, :, 0, half:]
    key = jnp.concatenate(
        [low_half * cosine - high_half * sine, high_half * cosine + low_half * sine], -1
    )
    fresh = jnp.stack([key, projected[:, :, 1]], 2).astype(BF16)
    new_kv = fresh.reshape(rows, steps, 2 * HEAD_SIZE)
    fresh_key = fresh[:, :, 0].astype(F32)
    fresh_value = fresh[:, :, 1].astype(F32)

    heads = queries.shape[2] // HEAD_SIZE
    q = queries.reshape(rows, steps * heads, HEAD_SIZE)
    top, total, gathered = cached_attention(q, k_cache, value_cache, kv_lengths)
    new_scores = jnp.einsum(
        "rqd,rtd->rqt", q, fresh[:, :, 0], preferred_element_type=F32
    ) * (1.0 / math.sqrt(HEAD_SIZE))
    step_of = jnp.arange(steps * heads, dtype=jnp.int32) // heads
    seen = jnp.arange(steps, dtype=jnp.int32)[None, :] <= step_of[:, None]
    new_scores = jnp.where(seen[None], new_scores, -jnp.inf)
    highest = jnp.maximum(top, jnp.max(new_scores, -1, keepdims=True))
    scale = jnp.exp(top - highest)
    new_weight = jnp.exp(new_scores - highest)
    total = total * scale + jnp.sum(new_weight, -1, keepdims=True)
    result = gathered * scale
    for s in range(steps):
        result = result + new_weight[:, :, s : s + 1] * fresh_value[:, s][:, None, :]
    attended = (result / total).astype(BF16).reshape(rows, steps, heads * HEAD_SIZE)
    return (new_kv, attended)


def solution(mesh):
    return jax.shard_map(
        per_device,
        mesh=mesh,
        in_specs=(
            P("dp", None, "tensor"),
            P(None, "tensor"),
            P("dp", "tensor", None),
            P("dp", None, "tensor"),
            P(),
            P("dp"),
            P("dp", None, "tensor"),
            P("dp", None, "tensor"),
            P("dp", None, "tensor"),
        ),
        out_specs=(P("dp", None, "tensor"), P("dp", None, "tensor")),
        check_vma=False,
    )
```

time: 393 us -> 110 us (0.28)
  the two profiles are of different devices: /device:TPU:32 before, /device:TPU:1 now
where the time goes in v1:
time: 110 us
  starting transfers between devices  39 us (35%)
  waiting for transfers between devices  32.9 us (30%)
  local copies, waits for them, and re-layouts  21.9 us (20%)
  matrix products  9.1 us (8%)
  other arithmetic  5.46 us (5%)
  between operations  1.4 us (1%)
    ppermute x6, waiting for transfers between devices, second_axis(): lax.ppermute(value, BOTH, pairs_of(lambda z, x, y, t, c: (z, x ^ (k if c...  12.4 us
    ppermute x2, waiting for transfers between devices, cross_z(): lax.ppermute(value, BOTH, pairs_of(lambda z, x, y, t, c: (z ^ c, x, y, t,...  11.2 us
    ppermute x9, starting transfers between devices, along_z(): lax.ppermute(value, BOTH, pairs_of(lambda z, x, y, t, c: (z, x, y, t ^ k,...  10.8 us
    ppermute x2, starting transfers between devices, cross_z(): lax.ppermute(value, BOTH, pairs_of(lambda z, x, y, t, c: (z ^ c, x, y, t,...  9.13 us
    ppermute x6, starting transfers between devices, second_axis(): lax.ppermute(value, BOTH, pairs_of(lambda z, x, y, t, c: (z, x ^ (k if c...  8.33 us
    ppermute x6, waiting for transfers between devices, first_axis(): lax.ppermute(value, BOTH, pairs_of(lambda z, x, y, t, c: (z, x ^ (0 if c...  7.53 us
    ppermute x6, starting transfers between devices, first_axis(): lax.ppermute(value, BOTH, pairs_of(lambda z, x, y, t, c: (z, x ^ (0 if c...  6.74 us
    ppermute x4, starting transfers between devices, swap_core(): lax.ppermute(value, BOTH, pairs_of(lambda z, x, y, t, c: (z, x, y, t, c ^...  3.93 us
  transfers between devices with their start and end apart: 27, of which 11 were waited for; matrix products, arithmetic and copies ran while one was open for 24% of the time, Pallas kernels for 0%

profile of v1, /device:TPU:1, one launch (start us, length us, event | category | flops | bytes accessed | tf_op | source)
XLA Modules:
  0.0 109.7 jit_solution(15253629666845694059)
XLA Ops:
  1.7 3.3 %collective-permute-start = (bf16[32,1024]{1,0:T(8,128)(2,1)S(1)}, bf16[32,1024]{1,0:T(8,128)(2,1)S(1)}, u32[]{:S(2)}, u32[]{:S(2)}) collective-permute-start(bf16[32,1024]{1,0:T(8,128)(2,1)S(1)} %reshape.269), channel_id=1, source_target_pairs={{0,1},{1,0},{2,3},{3,2},{4,5},{5,4},{6,7},{7,6},{8,9},{9,8},{10,11... | collective-permute-start | bytes 196616 | tf_op jit(solution)/shard_map/ppermute | solution.py:25
  7.1 2.4 %constant_dynamic-update-slice_fusion.7 = bf16[4,2048,128]{2,1,0:T(8,128)(2,1)} fusion(bf16[4,1024,128]{2,1,0:T(8,128)(2,1)} %param.11), kind=kLoop, calls=%fused_computation.101 | loop fusion | bytes 2097152
  19.0 2.9 %collective-permute-start.2 = (bf16[32,2048]{1,0:T(8,128)(2,1)}, bf16[32,2048]{1,0:T(8,128)(2,1)S(1)}, u32[]{:S(2)}, u32[]{:S(2)}) collective-permute-start(bf16[32,2048]{1,0:T(8,128)(2,1)} %constant_dynamic-update-slice_fusion), channel_id=1, source_target_pairs={{0,4},{1,5},{2,6},{3,7},{4,0},{5,1},{6,2},{7,3},{8,12},{9,13},{10,... | collective-permute-start | bytes 393224 | tf_op jit(solution)/shard_map/ppermute | solution.py:49
  22.6 7.2 %collective-permute-start.4 = (bf16[32,2048]{1,0:T(8,128)(2,1)}, bf16[32,2048]{1,0:T(8,128)(2,1)S(1)}, u32[]{:S(2)}, u32[]{:S(2)}) collective-permute-start(bf16[32,2048]{1,0:T(8,128)(2,1)} %constant_dynamic-update-slice_fusion), channel_id=1, source_target_pairs={{0,0},{1,129},{2,2},{3,131},{4,4},{5,133},{6,6},{7,135},{8,8},{9,1... | collective-permute-start | bytes 393224 | tf_op jit(solution)/shard_map/ppermute | solution.py:29
  30.6 6.8 %collective-permute-done.4 = bf16[32,2048]{1,0:T(8,128)(2,1)S(1)} collective-permute-done((bf16[32,2048]{1,0:T(8,128)(2,1)}, bf16[32,2048]{1,0:T(8,128)(2,1)S(1)}, u32[]{:S(2)}, u32[]{:S(2)}) %collective-permute-start.4) | collective-permute-done | bytes 131104 | tf_op jit(solution)/shard_map/ppermute | solution.py:29
  38.7 2.6 %collective-permute-start.6 = (bf16[32,2048]{1,0:T(8,128)(2,1)S(1)}, bf16[32,2048]{1,0:T(8,128)(2,1)S(1)}, u32[]{:S(2)}, u32[]{:S(2)}) collective-permute-start(bf16[32,2048]{1,0:T(8,128)(2,1)S(1)} %collective-permute-done.4), channel_id=1, source_target_pairs={{0,64},{1,17},{2,66},{3,19},{4,68},{5,21},{6,70},{7,23},{8,72},{9,... | collective-permute-start | bytes 393224 | tf_op jit(solution)/shard_map/ppermute | solution.py:33
  41.6 3.5 %collective-permute-done.6 = bf16[32,2048]{1,0:T(8,128)(2,1)S(1)} collective-permute-done((bf16[32,2048]{1,0:T(8,128)(2,1)S(1)}, bf16[32,2048]{1,0:T(8,128)(2,1)S(1)}, u32[]{:S(2)}, u32[]{:S(2)}) %collective-permute-start.6) | collective-permute-done | bytes 131104 | tf_op jit(solution)/shard_map/ppermute | solution.py:33
  45.1 2.3 %collective-permute-done.7 = bf16[32,2048]{1,0:T(8,128)(2,1)S(1)} collective-permute-done((bf16[32,2048]{1,0:T(8,128)(2,1)S(1)}, bf16[32,2048]{1,0:T(8,128)(2,1)S(1)}, u32[]{:S(2)}, u32[]{:S(2)}) %collective-permute-start.7) | collective-permute-done | bytes 131104 | tf_op jit(solution)/shard_map/ppermute | solution.py:33
  47.5 2.6 %collective-permute-start.11 = (bf16[128,2048]{1,0:T(8,128)(2,1)S(1)}, bf16[128,2048]{1,0:T(8,128)(2,1)S(1)}, u32[]{:S(2)}, u32[]{:S(2)}) collective-permute-start(bf16[128,2048]{1,0:T(8,128)(2,1)S(1)} %constant_dynamic-update-slice_fusion.2), channel_id=1, source_target_pairs={{0,24},{1,97},{2,26},{3,99},{4,28},{5,101},{6,30},{7,103},{8,16},{... | collective-permute-start | bytes 1572872 | tf_op jit(solution)/shard_map/ppermute | solution.py:41
  50.1 1.4 %collective-permute-start.10 = (bf16[128,2048]{1,0:T(8,128)(2,1)S(1)}, bf16[128,2048]{1,0:T(8,128)(2,1)S(1)}, u32[]{:S(2)}, u32[]{:S(2)}) collective-permute-start(bf16[128,2048]{1,0:T(8,128)(2,1)S(1)} %constant_dynamic-update-slice_fusion.2), channel_id=1, source_target_pairs={{0,16},{1,65},{2,18},{3,67},{4,20},{5,69},{6,22},{7,71},{8,24},{9,... | collective-permute-start | bytes 1572872 | tf_op jit(solution)/shard_map/ppermute | solution.py:41
  51.5 1.4 %constant_dynamic-update-slice_fusion.6 = bf16[4,2048,128]{2,1,0:T(8,128)(2,1)S(1)} fusion(bf16[4,2048,128]{2,1,0:T(8,128)(2,1)S(1)} %copy-done.1, bf16[4,1024,128]{2,1,0:T(8,128)(2,1)} %collective-permute-done.8), kind=kLoop, calls=%fused_computation.100 | loop fusion | bytes 2097152 | tf_op jit(solution)/shard_map/concatenate | solution.py:88
  53.4 9.0 %collective-permute-done.11 = bf16[128,2048]{1,0:T(8,128)(2,1)S(1)} collective-permute-done((bf16[128,2048]{1,0:T(8,128)(2,1)S(1)}, bf16[128,2048]{1,0:T(8,128)(2,1)S(1)}, u32[]{:S(2)}, u32[]{:S(2)}) %collective-permute-start.11) | collective-permute-done | bytes 524320 | tf_op jit(solution)/shard_map/ppermute | solution.py:41
  63.9 1.5 %collective-permute-start.14 = (bf16[128,128]{1,0:T(8,128)(2,1)S(1)}, bf16[128,128]{1,0:T(8,128)(2,1)S(1)}, u32[]{:S(2)}, u32[]{:S(2)}) collective-permute-start(bf16[128,128]{1,0:T(8,128)(2,1)S(1)} %get-tuple-element.27), channel_id=1, source_target_pairs={{0,6},{1,7},{2,4},{3,5},{4,2},{5,3},{6,0},{7,1},{8,14},{9,15},{10,... | collective-permute-start | bytes 98312 | tf_op jit(solution)/shard_map/ppermute | solution.py:49
  65.4 2.1 %collective-permute-start.12 = (bf16[128,128]{1,0:T(8,128)(2,1)S(1)}, bf16[128,128]{1,0:T(8,128)(2,1)S(1)}, u32[]{:S(2)}, u32[]{:S(2)}) collective-permute-start(bf16[128,128]{1,0:T(8,128)(2,1)S(1)} %get-tuple-element.26), channel_id=1, source_target_pairs={{0,2},{1,3},{2,0},{3,1},{4,6},{5,7},{6,4},{7,5},{8,10},{9,11},{10,... | collective-permute-start | bytes 98312 | tf_op jit(solution)/shard_map/ppermute | solution.py:49
  69.2 1.8 %collective-permute-start.17 = (bf16[128,128]{1,0:T(8,128)(2,1)S(1)}, bf16[128,128]{1,0:T(8,128)(2,1)S(1)}, u32[]{:S(2)}, u32[]{:S(2)}) collective-permute-start(bf16[128,128]{1,0:T(8,128)(2,1)S(1)} %fusion.37), channel_id=1, source_target_pairs={{0,6},{1,7},{2,4},{3,5},{4,2},{5,3},{6,0},{7,1},{8,14},{9,15},{10,... | collective-permute-start | bytes 98312 | tf_op jit(solution)/shard_map/ppermute | solution.py:49
  71.6 1.3 %collective-permute-start.15 = (bf16[128,128]{1,0:T(8,128)(2,1)S(1)}, bf16[128,128]{1,0:T(8,128)(2,1)S(1)}, u32[]{:S(2)}, u32[]{:S(2)}) collective-permute-start(bf16[128,128]{1,0:T(8,128)(2,1)S(1)} %fusion.37), channel_id=1, source_target_pairs={{0,2},{1,3},{2,0},{3,1},{4,6},{5,7},{6,4},{7,5},{8,10},{9,11},{10,... | collective-permute-start | bytes 98312 | tf_op jit(solution)/shard_map/ppermute | solution.py:49
  79.8 3.5 %collective-permute-start.21 = (bf16[128,512]{1,0:T(8,128)(2,1)S(1)}, bf16[128,512]{1,0:T(8,128)(2,1)S(1)}, u32[]{:S(2)}, u32[]{:S(2)}) collective-permute-start(bf16[128,512]{1,0:T(8,128)(2,1)S(1)} %get-tuple-element.11), channel_id=1, source_target_pairs={{0,16},{1,65},{2,18},{3,67},{4,20},{5,69},{6,22},{7,71},{8,24},{9,... | collective-permute-start | bytes 393224 | tf_op jit(solution)/shard_map/ppermute | solution.py:41
  85.7 2.7 %collective-permute-done.20 = bf16[128,512]{1,0:T(8,128)(2,1)S(1)} collective-permute-done((bf16[128,512]{1,0:T(8,128)(2,1)S(1)}, bf16[128,512]{1,0:T(8,128)(2,1)S(1)}, u32[]{:S(2)}, u32[]{:S(2)}) %collective-permute-start.20) | collective-permute-done | bytes 131104 | tf_op jit(solution)/shard_map/ppermute | solution.py:41
  88.5 2.0 %collective-permute-start.23 = (bf16[32,512]{1,0:T(8,128)(2,1)S(1)}, bf16[32,512]{1,0:T(8,128)(2,1)S(1)}, u32[]{:S(2)}, u32[]{:S(2)}) collective-permute-start(bf16[32,512]{1,0:T(8,128)(2,1)S(1)} %get-tuple-element.21), channel_id=1, source_target_pairs={{0,96},{1,25},{2,98},{3,27},{4,100},{5,29},{6,102},{7,31},{8,104},... | collective-permute-start | bytes 98312 | tf_op jit(solution)/shard_map/ppermute | solution.py:33
  93.7 1.9 %collective-permute-start.25 = (bf16[32,512]{1,0:T(8,128)(2,1)S(1)}, bf16[32,512]{1,0:T(8,128)(2,1)S(1)}, u32[]{:S(2)}, u32[]{:S(2)}) collective-permute-start(bf16[32,512]{1,0:T(8,128)(2,1)S(1)} %fusion.39), channel_id=1, source_target_pairs={{0,0},{1,129},{2,2},{3,131},{4,4},{5,133},{6,6},{7,135},{8,8},{9,1... | collective-permute-start | bytes 98312 | tf_op jit(solution)/shard_map/ppermute | solution.py:29
  96.4 1.4 %reshape.270 = bf16[32,8192]{1,0:T(8,128)(2,1)S(1)} reshape(bf16[32,4,2,1024]{3,2,1,0:T(2,128)(2,1)} %bitcast.11) | data formatting | bytes 1048576 | tf_op jit(solution)/shard_map/reshape | solution.py:160
  97.8 4.4 %collective-permute-done.25 = bf16[32,512]{1,0:T(8,128)(2,1)S(1)} collective-permute-done((bf16[32,512]{1,0:T(8,128)(2,1)S(1)}, bf16[32,512]{1,0:T(8,128)(2,1)S(1)}, u32[]{:S(2)}, u32[]{:S(2)}) %collective-permute-start.25) | collective-permute-done | bytes 32800 | tf_op jit(solution)/shard_map/ppermute | solution.py:29
  102.4 3.0 %fusion.62 = f32[32,256]{1,0:T(8,128)S(1)} fusion(bf16[32,8192]{1,0:T(8,128)(2,1)S(1)} %reshape.270, bf16[8192,256]{1,0:T(8,128)(2,1)} %param.10), kind=kOutput, calls=%fused_computation.145 | convolution fusion | flops 134217728 | bytes 4751360 | tf_op jit(solution)/shard_map/dot_general | solution.py:161
  107.0 2.0 %fusion.8 = bf16[16,16,128]{2,1,0:T(8,128)(2,1)S(1)} fusion(bf16[16,512,128]{2,1,0:T(8,128)(2,1)} %param.17, f32[16,16,512]{2,1,0:T(8,128)S(1)} %get-tuple-element.52, f32[16,16]{1,0:T(8,128)S(1)} %get-tuple-element.51, f32[16,16]{1,0:T(8,128)S(1)} %get-tuple-element.6, f32[16,128]{1,0:T(8,128)S(1)} %bitcast.183, f32[16,16]{1,0:T(8,128)S(1)} %bitcast.185, ...), kind=kOutput, calls=%fused_computation.17 | convolution fusion | flops 34045952 | bytes 2708480 | tf_op jit(solution)/shard_map/rqj,rjd->rqd/dot_general | solution.py:61
  (163 shorter events, 35.1 us)
Async XLA Ops:
  1.7 16.7 %collective-permute-start = (bf16[32,1024]{1,0:T(8,128)(2,1)S(1)}, bf16[32,1024]{1,0:T(8,128)(2,1)S(1)}, u32[]{:S(2)}, u32[]{:S(2)}) collective-permute-start(bf16[32,1024]{1,0:T(8,128)(2,1)S(1)} %reshape.269), channel_id=1, source_target_pairs={{0,1},{1,0},{2,3},{3,2},{4,5},{5,4},{6,7},{7,6},{8,9},{9,8},{10,11... | collective-permute-start | bytes 196616 | tf_op jit(solution)/shard_map/ppermute | solution.py:25
  5.0 46.5 %collective-permute-start.8 = (bf16[4,1024,128]{2,1,0:T(8,128)(2,1)}, bf16[4,1024,128]{2,1,0:T(8,128)(2,1)}, u32[]{:S(2)}, u32[]{:S(2)}) collective-permute-start(bf16[4,1024,128]{2,1,0:T(8,128)(2,1)} %param.11), channel_id=1, source_target_pairs={{0,1},{1,0},{2,3},{3,2},{4,5},{5,4},{6,7},{7,6},{8,9},{9,8},{10,11... | collective-permute-start | bytes 3145736 | tf_op jit(solution)/shard_map/ppermute | solution.py:25
  5.1 17.5 %collective-permute-start.18 = (bf16[4,64,256]{2,1,0:T(8,128)(2,1)}, bf16[4,64,256]{2,1,0:T(8,128)(2,1)S(1)}, u32[]{:S(2)}, u32[]{:S(2)}) collective-permute-start(bf16[4,64,256]{2,1,0:T(8,128)(2,1)} %param.12), channel_id=1, source_target_pairs={{0,1},{1,0},{2,3},{3,2},{4,5},{5,4},{6,7},{7,6},{8,9},{9,8},{10,11... | collective-permute-start | bytes 393224 | tf_op jit(solution)/shard_map/ppermute | solution.py:25
  19.0 11.5 %collective-permute-start.1 = (bf16[32,2048]{1,0:T(8,128)(2,1)}, bf16[32,2048]{1,0:T(8,128)(2,1)S(1)}, u32[]{:S(2)}, u32[]{:S(2)}) collective-permute-start(bf16[32,2048]{1,0:T(8,128)(2,1)} %constant_dynamic-update-slice_fusion), channel_id=1, source_target_pairs={{0,2},{1,3},{2,0},{3,1},{4,6},{5,7},{6,4},{7,5},{8,10},{9,11},{10,... | collective-permute-start | bytes 393224 | tf_op jit(solution)/shard_map/ppermute | solution.py:49
  19.0 22.4 %collective-permute-start.2 = (bf16[32,2048]{1,0:T(8,128)(2,1)}, bf16[32,2048]{1,0:T(8,128)(2,1)S(1)}, u32[]{:S(2)}, u32[]{:S(2)}) collective-permute-start(bf16[32,2048]{1,0:T(8,128)(2,1)} %constant_dynamic-update-slice_fusion), channel_id=1, source_target_pairs={{0,4},{1,5},{2,6},{3,7},{4,0},{5,1},{6,2},{7,3},{8,12},{9,13},{10,... | collective-permute-start | bytes 393224 | tf_op jit(solution)/shard_map/ppermute | solution.py:49
  21.9 19.6 %collective-permute-start.3 = (bf16[32,2048]{1,0:T(8,128)(2,1)}, bf16[32,2048]{1,0:T(8,128)(2,1)S(1)}, u32[]{:S(2)}, u32[]{:S(2)}) collective-permute-start(bf16[32,2048]{1,0:T(8,128)(2,1)} %constant_dynamic-update-slice_fusion), channel_id=1, source_target_pairs={{0,6},{1,7},{2,4},{3,5},{4,2},{5,3},{6,0},{7,1},{8,14},{9,15},{10,... | collective-permute-start | bytes 393224 | tf_op jit(solution)/shard_map/ppermute | solution.py:49
  22.6 14.8 %collective-permute-start.4 = (bf16[32,2048]{1,0:T(8,128)(2,1)}, bf16[32,2048]{1,0:T(8,128)(2,1)S(1)}, u32[]{:S(2)}, u32[]{:S(2)}) collective-permute-start(bf16[32,2048]{1,0:T(8,128)(2,1)} %constant_dynamic-update-slice_fusion), channel_id=1, source_target_pairs={{0,0},{1,129},{2,2},{3,131},{4,4},{5,133},{6,6},{7,135},{8,8},{9,1... | collective-permute-start | bytes 393224 | tf_op jit(solution)/shard_map/ppermute | solution.py:29
  37.5 4.1 %collective-permute-start.5 = (bf16[32,2048]{1,0:T(8,128)(2,1)S(1)}, bf16[32,2048]{1,0:T(8,128)(2,1)S(1)}, u32[]{:S(2)}, u32[]{:S(2)}) collective-permute-start(bf16[32,2048]{1,0:T(8,128)(2,1)S(1)} %collective-permute-done.4), channel_id=1, source_target_pairs={{0,32},{1,9},{2,34},{3,11},{4,36},{5,13},{6,38},{7,15},{8,40},{9,1... | collective-permute-start | bytes 393224 | tf_op jit(solution)/shard_map/ppermute | solution.py:33
  38.7 6.4 %collective-permute-start.6 = (bf16[32,2048]{1,0:T(8,128)(2,1)S(1)}, bf16[32,2048]{1,0:T(8,128)(2,1)S(1)}, u32[]{:S(2)}, u32[]{:S(2)}) collective-permute-start(bf16[32,2048]{1,0:T(8,128)(2,1)S(1)} %collective-permute-done.4), channel_id=1, source_target_pairs={{0,64},{1,17},{2,66},{3,19},{4,68},{5,21},{6,70},{7,23},{8,72},{9,... | collective-permute-start | bytes 393224 | tf_op jit(solution)/shard_map/ppermute | solution.py:33
  41.4 6.1 %collective-permute-start.7 = (bf16[32,2048]{1,0:T(8,128)(2,1)S(1)}, bf16[32,2048]{1,0:T(8,128)(2,1)S(1)}, u32[]{:S(2)}, u32[]{:S(2)}) collective-permute-start(bf16[32,2048]{1,0:T(8,128)(2,1)S(1)} %collective-permute-done.4), channel_id=1, source_target_pairs={{0,96},{1,25},{2,98},{3,27},{4,100},{5,29},{6,102},{7,31},{8,104},... | collective-permute-start | bytes 393224 | tf_op jit(solution)/shard_map/ppermute | solution.py:33
  47.5 14.9 %collective-permute-start.11 = (bf16[128,2048]{1,0:T(8,128)(2,1)S(1)}, bf16[128,2048]{1,0:T(8,128)(2,1)S(1)}, u32[]{:S(2)}, u32[]{:S(2)}) collective-permute-start(bf16[128,2048]{1,0:T(8,128)(2,1)S(1)} %constant_dynamic-update-slice_fusion.2), channel_id=1, source_target_pairs={{0,24},{1,97},{2,26},{3,99},{4,28},{5,101},{6,30},{7,103},{8,16},{... | collective-permute-start | bytes 1572872 | tf_op jit(solution)/shard_map/ppermute | solution.py:41
  50.1 12.7 %collective-permute-start.10 = (bf16[128,2048]{1,0:T(8,128)(2,1)S(1)}, bf16[128,2048]{1,0:T(8,128)(2,1)S(1)}, u32[]{:S(2)}, u32[]{:S(2)}) collective-permute-start(bf16[128,2048]{1,0:T(8,128)(2,1)S(1)} %constant_dynamic-update-slice_fusion.2), channel_id=1, source_target_pairs={{0,16},{1,65},{2,18},{3,67},{4,20},{5,69},{6,22},{7,71},{8,24},{9,... | collective-permute-start | bytes 1572872 | tf_op jit(solution)/shard_map/ppermute | solution.py:41
  51.5 11.8 %collective-permute-start.9 = (bf16[128,2048]{1,0:T(8,128)(2,1)S(1)}, bf16[128,2048]{1,0:T(8,128)(2,1)S(1)}, u32[]{:S(2)}, u32[]{:S(2)}) collective-permute-start(bf16[128,2048]{1,0:T(8,128)(2,1)S(1)} %constant_dynamic-update-slice_fusion.2), channel_id=1, source_target_pairs={{0,8},{1,33},{2,10},{3,35},{4,12},{5,37},{6,14},{7,39},{8,0},{9,41... | collective-permute-start | bytes 1572872 | tf_op jit(solution)/shard_map/ppermute | solution.py:41
  63.9 4.7 %collective-permute-start.14 = (bf16[128,128]{1,0:T(8,128)(2,1)S(1)}, bf16[128,128]{1,0:T(8,128)(2,1)S(1)}, u32[]{:S(2)}, u32[]{:S(2)}) collective-permute-start(bf16[128,128]{1,0:T(8,128)(2,1)S(1)} %get-tuple-element.27), channel_id=1, source_target_pairs={{0,6},{1,7},{2,4},{3,5},{4,2},{5,3},{6,0},{7,1},{8,14},{9,15},{10,... | collective-permute-start | bytes 98312 | tf_op jit(solution)/shard_map/ppermute | solution.py:49
  65.4 3.9 %collective-permute-start.13 = (bf16[128,128]{1,0:T(8,128)(2,1)S(1)}, bf16[128,128]{1,0:T(8,128)(2,1)S(1)}, u32[]{:S(2)}, u32[]{:S(2)}) collective-permute-start(bf16[128,128]{1,0:T(8,128)(2,1)S(1)} %get-tuple-element.28), channel_id=1, source_target_pairs={{0,4},{1,5},{2,6},{3,7},{4,0},{5,1},{6,2},{7,3},{8,12},{9,13},{10,... | collective-permute-start | bytes 98312 | tf_op jit(solution)/shard_map/ppermute | solution.py:49
  65.4 3.9 %collective-permute-start.12 = (bf16[128,128]{1,0:T(8,128)(2,1)S(1)}, bf16[128,128]{1,0:T(8,128)(2,1)S(1)}, u32[]{:S(2)}, u32[]{:S(2)}) collective-permute-start(bf16[128,128]{1,0:T(8,128)(2,1)S(1)} %get-tuple-element.26), channel_id=1, source_target_pairs={{0,2},{1,3},{2,0},{3,1},{4,6},{5,7},{6,4},{7,5},{8,10},{9,11},{10,... | collective-permute-start | bytes 98312 | tf_op jit(solution)/shard_map/ppermute | solution.py:49
  69.2 5.7 %collective-permute-start.17 = (bf16[128,128]{1,0:T(8,128)(2,1)S(1)}, bf16[128,128]{1,0:T(8,128)(2,1)S(1)}, u32[]{:S(2)}, u32[]{:S(2)}) collective-permute-start(bf16[128,128]{1,0:T(8,128)(2,1)S(1)} %fusion.37), channel_id=1, source_target_pairs={{0,6},{1,7},{2,4},{3,5},{4,2},{5,3},{6,0},{7,1},{8,14},{9,15},{10,... | collective-permute-start | bytes 98312 | tf_op jit(solution)/shard_map/ppermute | solution.py:49
  71.0 3.9 %collective-permute-start.16 = (bf16[128,128]{1,0:T(8,128)(2,1)S(1)}, bf16[128,128]{1,0:T(8,128)(2,1)S(1)}, u32[]{:S(2)}, u32[]{:S(2)}) collective-permute-start(bf16[128,128]{1,0:T(8,128)(2,1)S(1)} %fusion.37), channel_id=1, source_target_pairs={{0,4},{1,5},{2,6},{3,7},{4,0},{5,1},{6,2},{7,3},{8,12},{9,13},{10,... | collective-permute-start | bytes 98312 | tf_op jit(solution)/shard_map/ppermute | solution.py:49
  79.8 5.8 %collective-permute-start.21 = (bf16[128,512]{1,0:T(8,128)(2,1)S(1)}, bf16[128,512]{1,0:T(8,128)(2,1)S(1)}, u32[]{:S(2)}, u32[]{:S(2)}) collective-permute-start(bf16[128,512]{1,0:T(8,128)(2,1)S(1)} %get-tuple-element.11), channel_id=1, source_target_pairs={{0,16},{1,65},{2,18},{3,67},{4,20},{5,69},{6,22},{7,71},{8,24},{9,... | collective-permute-start | bytes 393224 | tf_op jit(solution)/shard_map/ppermute | solution.py:41
  83.3 5.0 %collective-permute-start.20 = (bf16[128,512]{1,0:T(8,128)(2,1)S(1)}, bf16[128,512]{1,0:T(8,128)(2,1)S(1)}, u32[]{:S(2)}, u32[]{:S(2)}) collective-permute-start(bf16[128,512]{1,0:T(8,128)(2,1)S(1)} %get-tuple-element.12), channel_id=1, source_target_pairs={{0,24},{1,97},{2,26},{3,99},{4,28},{5,101},{6,30},{7,103},{8,16},{... | collective-permute-start | bytes 393224 | tf_op jit(solution)/shard_map/ppermute | solution.py:41
  84.2 4.2 %collective-permute-start.19 = (bf16[128,512]{1,0:T(8,128)(2,1)S(1)}, bf16[128,512]{1,0:T(8,128)(2,1)S(1)}, u32[]{:S(2)}, u32[]{:S(2)}) collective-permute-start(bf16[128,512]{1,0:T(8,128)(2,1)S(1)} %get-tuple-element.10), channel_id=1, source_target_pairs={{0,8},{1,33},{2,10},{3,35},{4,12},{5,37},{6,14},{7,39},{8,0},{9,41... | collective-permute-start | bytes 393224 | tf_op jit(solution)/shard_map/ppermute | solution.py:41
  88.4 4.5 %collective-permute-start.24 = (bf16[32,512]{1,0:T(8,128)(2,1)S(1)}, bf16[32,512]{1,0:T(8,128)(2,1)S(1)}, u32[]{:S(2)}, u32[]{:S(2)}) collective-permute-start(bf16[32,512]{1,0:T(8,128)(2,1)S(1)} %get-tuple-element.20), channel_id=1, source_target_pairs={{0,64},{1,17},{2,66},{3,19},{4,68},{5,21},{6,70},{7,23},{8,72},{9,... | collective-permute-start | bytes 98312 | tf_op jit(solution)/shard_map/ppermute | solution.py:33
  88.5 4.4 %collective-permute-start.23 = (bf16[32,512]{1,0:T(8,128)(2,1)S(1)}, bf16[32,512]{1,0:T(8,128)(2,1)S(1)}, u32[]{:S(2)}, u32[]{:S(2)}) collective-permute-start(bf16[32,512]{1,0:T(8,128)(2,1)S(1)} %get-tuple-element.21), channel_id=1, source_target_pairs={{0,96},{1,25},{2,98},{3,27},{4,100},{5,29},{6,102},{7,31},{8,104},... | collective-permute-start | bytes 98312 | tf_op jit(solution)/shard_map/ppermute | solution.py:33
  93.7 8.6 %collective-permute-start.25 = (bf16[32,512]{1,0:T(8,128)(2,1)S(1)}, bf16[32,512]{1,0:T(8,128)(2,1)S(1)}, u32[]{:S(2)}, u32[]{:S(2)}) collective-permute-start(bf16[32,512]{1,0:T(8,128)(2,1)S(1)} %fusion.39), channel_id=1, source_target_pairs={{0,0},{1,129},{2,2},{3,131},{4,4},{5,133},{6,6},{7,135},{8,8},{9,1... | collective-permute-start | bytes 98312 | tf_op jit(solution)/shard_map/ppermute | solution.py:29
  (21 other events, 204.2 us)

commit v2 on v1

v2 whole, which is shorter than its diff:
```python
import math

import jax
import jax.numpy as jnp
from jax import lax
from jax.experimental import pallas as pl
from jax.experimental.pallas import tpu as pltpu
from jax.sharding import PartitionSpec as P

HEAD_SIZE = 128
F32 = jnp.float32
BF16 = jnp.bfloat16
BOTH = ("dp", "tensor")


def pairs_of(move):
    pairs = []
    for d in range(32):
        for j in range(8):
            z, x, y, t, c = d // 16, d // 4 % 4, d % 4, j // 2, j % 2
            z, x, y, t, c = move(z, x, y, t, c)
            pairs.append((d * 8 + j, (z * 16 + x * 4 + y) * 8 + t * 2 + c))
    return pairs


def swap_core(value):
    return lax.ppermute(value, BOTH, pairs_of(lambda z, x, y, t, c: (z, x, y, t, c ^ 1)))


def cross_z(value):
    return lax.ppermute(value, BOTH, pairs_of(lambda z, x, y, t, c: (z ^ c, x, y, t, c)))


def first_axis(value, k):
    return lax.ppermute(
        value,
        BOTH,
        pairs_of(lambda z, x, y, t, c: (z, x ^ (0 if c else k), y ^ (k if c else 0), t, c)),
    )


def second_axis(value, k):
    return lax.ppermute(
        value,
        BOTH,
        pairs_of(lambda z, x, y, t, c: (z, x ^ (k if c else 0), y ^ (0 if c else k), t, c)),
    )


def along_z(value, k):
    return lax.ppermute(value, BOTH, pairs_of(lambda z, x, y, t, c: (z, x, y, t ^ k, c)))


def swap_z(value):
    return lax.ppermute(value, BOTH, pairs_of(lambda z, x, y, t, c: (z ^ 1, x, y, t, c)))


def hbm():
    return pl.BlockSpec(memory_space=pl.ANY)


def vmem():
    return pl.BlockSpec(memory_space=pltpu.VMEM)


def smem():
    return pl.BlockSpec(memory_space=pltpu.SMEM)


def mask_kernel(
    groups_ref, first_ref, ids_ref, up_own_ref, up_other_ref, own_ref, after_ref,
    code_ref, up_ref, same_ref,
):
    first = first_ref[0]
    same_ref[...] = own_ref[...]
    for k2 in range(4):
        for k1 in range(4):
            code_ref[k2, 32 * k1 : 32 * k1 + 32, :] = ids_ref[groups_ref[4 * k2 + k1]] - first
    up_ref[...] = jnp.zeros_like(up_ref)
    for a in range(up_own_ref.shape[0]):
        for n, ref in enumerate((up_own_ref, up_other_ref)):
            at = 2 * HEAD_SIZE * n
            up_ref[128 * a : 128 * a + 64, at : at + 128] = ref[a, :, :128]
            up_ref[128 * a + 64 : 128 * a + 128, at + 128 : at + 256] = ref[a, :, 128:]


def make_masks(groups, first, ids_wide, up_own, up_other, own, after):
    owned = up_own.shape[0]
    return pl.pallas_call(
        mask_kernel,
        out_shape=(
            jax.ShapeDtypeStruct((4, 128, 128), jnp.int32),
            jax.ShapeDtypeStruct((owned * 128, 512), BF16),
            jax.ShapeDtypeStruct(own.shape, BF16),
        ),
        in_specs=[smem(), smem(), vmem(), vmem(), vmem(), vmem(), hbm()],
        out_specs=(vmem(), vmem(), vmem()),
        name="masks",
        cost_estimate=pl.CostEstimate(flops=1_000_000, bytes_accessed=2_000_000, transcendentals=0),
    )(groups, first, ids_wide, up_own, up_other, own, after)


def down_kernel(x_ref, own_ref, other_ref, code_ref, *rest):
    wide_ref, narrow_ref = rest[-2:]
    rows = x_ref.shape[0] * x_ref.shape[2]
    left = x_ref[:, 0].reshape(rows, x_ref.shape[3])
    right = x_ref[:, 1].reshape(rows, x_ref.shape[3])
    code = code_ref[...]
    total = jnp.zeros(wide_ref.shape, F32)
    for a in range(own_ref.shape[0]):
        product = jnp.dot(left, own_ref[a], preferred_element_type=F32)
        product = product + jnp.dot(right, other_ref[a], preferred_element_type=F32)
        total = jnp.where(code == a, product, total)
    wide_ref[...] = total
    narrow_ref[...] = total.astype(BF16)


def down_block(x, own, other, code, after=()):
    return pl.pallas_call(
        down_kernel,
        out_shape=(
            jax.ShapeDtypeStruct((128, 128), F32),
            jax.ShapeDtypeStruct((128, 128), BF16),
        ),
        in_specs=[vmem()] * 4 + [hbm()] * len(after),
        out_specs=(vmem(), vmem()),
        name="down",
        cost_estimate=pl.CostEstimate(
            flops=2 * 128 * 2048 * 512, bytes_accessed=1_000_000, transcendentals=0
        ),
    )(x, own, other, code, *after)


def up_kernel(t_ref, r0, r1, r2, r3, code_ref, up_ref, d0, d1, d2, d3, held):
    t = t_ref[0]
    for m, ref in enumerate((r0, r1, r2, r3)):
        held[m] = ref[...]
    for k2, out in enumerate((d0, d1, d2, d3)):
        low = held[jnp.bitwise_xor(t, k2)]
        code = code_ref[k2]
        zero = jnp.zeros_like(low)
        spread = jnp.concatenate(
            [jnp.where(code == a, low.astype(F32), 0.0).astype(BF16) for a in range(up_ref.shape[0] // 128)], 1
        )
        out[...] = jnp.dot(spread, up_ref[...], preferred_element_type=F32).astype(BF16)


def up_blocks(t, slots, code, up):
    return pl.pallas_call(
        up_kernel,
        out_shape=[jax.ShapeDtypeStruct((128, 512), BF16)] * 4,
        in_specs=[smem()] + [vmem()] * 6,
        out_specs=[vmem()] * 4,
        scratch_shapes=[pltpu.VMEM((4, 128, 128), BF16)],
        name="up",
        cost_estimate=pl.CostEstimate(
            flops=2 * 512 * 512 * 512, bytes_accessed=2_000_000, transcendentals=0
        ),
    )(t, *slots, code, up)


def attention_kernel(lengths_ref, q_ref, k_ref, v_ref, after_ref, top_ref, total_ref, sum_ref):
    step = pl.program_id(0)
    per = q_ref.shape[0]
    for n in range(per):
        length = lengths_ref[step * per + n]
        scores = lax.dot_general(
            q_ref[n], k_ref[n], (((1,), (1,)), ((), ())), preferred_element_type=F32
        ) * (1.0 / math.sqrt(HEAD_SIZE))
        spot = lax.broadcasted_iota(jnp.int32, scores.shape, 1)
        scores = jnp.where(spot < length, scores, -jnp.inf)
        top = jnp.max(scores, -1, keepdims=True)
        weight = jnp.exp(scores - top)
        total = jnp.sum(weight, -1, keepdims=True)
        top_ref[n] = jnp.broadcast_to(top, top_ref.shape[1:])
        total_ref[n] = jnp.broadcast_to(total, total_ref.shape[1:])
        sum_ref[n] = jnp.dot(weight.astype(BF16), v_ref[n], preferred_element_type=F32)


def cached_attention(lengths, queries, k_cache, value_cache, after):
    rows, context, _ = k_cache.shape
    heads = queries.shape[1]
    per = 4
    wide = jax.ShapeDtypeStruct((rows, heads, HEAD_SIZE), F32)
    block = lambda n: pl.BlockSpec((per, n, HEAD_SIZE), lambda i: (i, 0, 0))
    return pl.pallas_call(
        attention_kernel,
        grid=(rows // per,),
        out_shape=(wide, wide, wide),
        in_specs=[smem(), block(heads), block(context), block(context), hbm()],
        out_specs=(block(heads), block(heads), block(heads)),
        name="cached",
        cost_estimate=pl.CostEstimate(
            flops=4 * rows * heads * context * HEAD_SIZE,
            bytes_accessed=4 * rows * context * HEAD_SIZE,
            transcendentals=rows * heads * context,
        ),
    )(lengths, queries, k_cache, value_cache, after)


def base_kernel(j_ref, s0, s1, s2, s3, p_ref, o_ref, w_ref, out_ref, held):
    step = pl.program_id(0)

    @pl.when(step == 0)
    def _():
        for m, ref in enumerate((s0, s1, s2, s3)):
            held[2 * m] = ref[...]
            held[2 * m + 1] = p_ref[1] if m == 0 else o_ref[m - 1]
        out_ref[...] = jnp.zeros_like(out_ref)

    out_ref[...] += jnp.dot(
        held[jnp.bitwise_xor(j_ref[0], step)], w_ref[...], preferred_element_type=F32
    )


def base_projection(j, slots, pair, others, weight):
    group, width = slots[0].shape
    columns = weight.shape[1]
    whole = lambda x: pl.BlockSpec(x.shape, lambda i: (0,) * x.ndim)
    return pl.pallas_call(
        base_kernel,
        grid=(8,),
        out_shape=jax.ShapeDtypeStruct((group, columns), F32),
        in_specs=[smem()]
        + [whole(x) for x in (*slots, pair, others)]
        + [pl.BlockSpec((width, columns), lambda i: (i, 0))],
        out_specs=pl.BlockSpec((group, columns), lambda i: (0, 0)),
        scratch_shapes=[pltpu.VMEM((8, group, width), BF16)],
        name="base",
        cost_estimate=pl.CostEstimate(
            flops=2 * group * 8 * width * columns,
            bytes_accessed=2 * 8 * width * columns,
            transcendentals=0,
        ),
    )(j, *slots, pair, others, weight)


def final_kernel(
    base_ref, kept_ref, came_ref, cos_ref, sin_ref, q_ref, top_ref, total_ref, sum_ref,
    new_ref, out_ref, held, result,
):
    rows, queries, _ = q_ref.shape
    heads = queries // 2
    update = kept_ref[...].astype(F32) + came_ref[...].astype(F32)
    projected = base_ref[...] + update
    key = projected[:, :HEAD_SIZE]
    turned = pltpu.roll(key, HEAD_SIZE // 2, 1)
    key = key * cos_ref[...] + turned * sin_ref[...]
    fresh = jnp.concatenate([key, projected[:, HEAD_SIZE:]], 1).astype(BF16)
    held[0] = fresh[:, :HEAD_SIZE].astype(F32)
    held[1] = fresh[:, HEAD_SIZE:].astype(F32)
    q = q_ref[...].astype(F32)
    scale = 1.0 / math.sqrt(HEAD_SIZE)
    keys = [held[0, pl.ds(s, rows, stride=2), :] for s in range(2)]
    values = [held[1, pl.ds(s, rows, stride=2), :] for s in range(2)]
    scores = [jnp.sum(q * k[:, None, :], -1, keepdims=True) * scale for k in keys]
    second = lax.broadcasted_iota(jnp.int32, scores[1].shape, 1) >= heads
    scores[1] = jnp.where(second, scores[1], -jnp.inf)
    top = top_ref[...]
    highest = jnp.maximum(top, jnp.maximum(scores[0], scores[1]))
    old = jnp.exp(top - highest)
    new = [jnp.exp(s - highest) for s in scores]
    total = total_ref[...] * old + new[0] + new[1]
    mixed = sum_ref[...] * old + new[0] * values[0][:, None, :] + new[1] * values[1][:, None, :]
    result[...] = (mixed / total).reshape(rows * queries, HEAD_SIZE)
    new_ref[:, :, :HEAD_SIZE] = jnp.stack(keys, 1).astype(BF16)
    new_ref[:, :, HEAD_SIZE:] = jnp.stack(values, 1).astype(BF16)
    for g in range(heads):
        both = [result[pl.ds(s * heads + g, rows, stride=queries), :] for s in range(2)]
        out_ref[:, :, HEAD_SIZE * g : HEAD_SIZE * (g + 1)] = jnp.stack(both, 1).astype(BF16)


def final_merge(base, kept, came, cosine, sine, q, top, total, gathered):
    rows, queries, _ = q.shape
    group = 2 * rows
    return pl.pallas_call(
        final_kernel,
        out_shape=(
            jax.ShapeDtypeStruct((rows, 2, 2 * HEAD_SIZE), BF16),
            jax.ShapeDtypeStruct((rows, 2, queries // 2 * HEAD_SIZE), BF16),
        ),
        in_specs=[vmem()] * 9,
        out_specs=(vmem(), vmem()),
        scratch_shapes=[
            pltpu.VMEM((2, group, HEAD_SIZE), F32),
            pltpu.VMEM((rows * queries, HEAD_SIZE), F32),
        ],
        name="merge",
        cost_estimate=pl.CostEstimate(flops=2_000_000, bytes_accessed=1_000_000, transcendentals=1000),
    )(base, kept, came, cosine, sine, q, top, total, gathered)


def per_device(
    hidden_rows,
    key_value_weight,
    adapter_down_weight,
    adapter_up_weight,
    adapter_ids,
    kv_lengths,
    queries,
    k_cache,
    value_cache,
):
    rows, steps, width = hidden_rows.shape
    owned = adapter_down_weight.shape[0]
    group = rows * steps
    me = lax.axis_index("dp")
    j = lax.axis_index("tensor")
    t, c = j // 2, j % 2

    own = lax.optimization_barrier(hidden_rows.reshape(group, width))
    pair = jnp.stack([own, swap_core(own)])

    start = cross_z(pair)
    down_other = swap_core(adapter_down_weight)
    up_other = swap_core(adapter_up_weight)
    line = jnp.stack([start] + [first_axis(start, k) for k in (1, 2, 3)])
    blocks = {0: line}
    for k in (1, 3, 2):
        blocks[k] = second_axis(line, k)

    k2 = jnp.arange(4, dtype=jnp.int32)[:, None]
    k1 = jnp.arange(4, dtype=jnp.int32)[None, :]
    groups = me ^ (16 * c) ^ jnp.where(c == 0, 4 * k1 + k2, 4 * k2 + k1)
    ids_wide = jnp.broadcast_to(
        jnp.repeat(adapter_ids, steps).reshape(-1, group, 1), (32, group, 128)
    )
    code, up, same = make_masks(
        groups.reshape(16),
        (me * owned).reshape(1),
        ids_wide,
        adapter_up_weight,
        up_other,
        own,
        line,
    )

    q = queries.reshape(rows, -1, HEAD_SIZE)
    top, total, gathered = cached_attention(kv_lengths, q, k_cache, value_cache, line)
    chips = [same] + [along_z(same, m) for m in (1, 2, 3)]

    wide, narrow = [], []
    for k in range(4):
        after = (top, *chips[1:]) if k == 2 else ()
        w, n = down_block(blocks[k], adapter_down_weight, down_other, code[k], after)
        wide.append(w)
        narrow.append(n)
    wide, narrow = jnp.stack(wide), jnp.stack(narrow)

    mine = lax.dynamic_index_in_dim(wide, t, 0, keepdims=False)
    for m in (1, 2, 3):
        sent = lax.dynamic_index_in_dim(narrow, t ^ m, 0, keepdims=False)
        mine = mine + along_z(sent, m).astype(F32)
    mine = mine.astype(BF16)
    slots = [mine] + [along_z(mine, m) for m in (1, 2, 3)]
    delta = up_blocks(t.reshape(1), slots, code, up)

    back = delta[0]
    for k in (1, 3, 2):
        back = back + second_axis(delta[k], k)
    back = back.reshape(4, group, 4 * HEAD_SIZE)
    home = back[0]
    for k in (1, 3, 2):
        home = home + first_axis(back[k], k)
    here, there = home[:, : 2 * HEAD_SIZE], swap_core(home[:, 2 * HEAD_SIZE :])
    kept = jnp.where(c == 0, here, there)
    came = swap_z(jnp.where(c == 0, there, here))

    others = swap_core(jnp.stack(chips[1:]))
    base = base_projection(j.reshape(1), chips, pair, others, key_value_weight)

    half = HEAD_SIZE // 2
    frequency = jnp.exp(jnp.arange(half, dtype=F32) * (-2.0 * math.log(500000.0) / HEAD_SIZE))
    positions = (kv_lengths[:, None] + jnp.arange(steps, dtype=jnp.int32)[None, :]).reshape(group)
    angles = positions.astype(F32)[:, None] * frequency
    cosine, sine = jnp.cos(angles), jnp.sin(angles)
    cosine = jnp.concatenate([cosine, cosine], 1)
    sine = jnp.concatenate([-sine, sine], 1)
    return final_merge(base, kept, came, cosine, sine, q, top, total, gathered)


def solution(mesh):
    return jax.shard_map(
        per_device,
        mesh=mesh,
        in_specs=(
            P("dp", None, "tensor"),
            P(None, "tensor"),
            P("dp", "tensor", None),
            P("dp", None, "tensor"),
            P(),
            P("dp"),
            P("dp", None, "tensor"),
            P("dp", None, "tensor"),
            P("dp", None, "tensor"),
        ),
        out_specs=(P("dp", None, "tensor"), P("dp", None, "tensor")),
        check_vma=False,
    )
```

time: 110 us -> 113 us (1.027)
  Pallas kernels: 0 us -> 31.2 us
  local copies, waits for them, and re-layouts: 21.9 us -> 10.2 us
  waiting for transfers between devices: 32.9 us -> 22 us
  matrix products: 9.1 us -> 0 us
  starting transfers between devices: 39 us -> 44 us
  other arithmetic: 5.46 us -> 3.52 us
    pallas_call x0 -> x9, Pallas kernels: none -> 31.2 us  [the longest x4 12.2 us: down_block(): pl.pallas_call(down_kernel, out_shape=(jax.ShapeDtypeStruct((128, 128), F...]
    dot_general x10 -> x0, matrix products: 9.1 us -> none  [the longest x1 3.01 us: per_device(): base = jnp.dot(full, key_value_weight, preferred_element_type=F32)]
    ppermute x2 -> x1, waiting for transfers between devices: 11.2 us -> 2.63 us  [cross_z(): lax.ppermute(value, BOTH, pairs_of(lambda z, x, y, t, c: (z ^ c, x, y, t,...]
    ppermute x6, waiting for transfers between devices: 12.4 us -> 4.51 us  [second_axis(): lax.ppermute(value, BOTH, pairs_of(lambda z, x, y, t, c: (z, x ^ (k if c...]
    ppermute x0 -> x1, starting transfers between devices: none -> 4.77 us  [swap_z(): lax.ppermute(value, BOTH, pairs_of(lambda z, x, y, t, c: (z ^ 1, x, y, t,...]
    ppermute x9, waiting for transfers between devices: 1.69 us -> 6.02 us  [along_z(): lax.ppermute(value, BOTH, pairs_of(lambda z, x, y, t, c: (z, x, y, t ^ k,...]
    ppermute x4 -> x5, starting transfers between devices: 3.93 us -> 7.7 us  [swap_core(): lax.ppermute(value, BOTH, pairs_of(lambda z, x, y, t, c: (z, x, y, t, c ^...]
    dynamic_update_slice x4 -> x0, local copies, waits for them, and re-layouts: 3.2 us -> none  [per_device(): full = lax.dynamic_update_slice(full, both[None], (t ^ m, 0, 0, 0))]
  transfers between devices with their start and end apart: 27 -> 28, of which waited for: 11 -> 13; matrix products, arithmetic and copies ran while one was open for 24% -> 7% of each run, Pallas kernels for 0% -> 21%
where the time goes in v2:
time: 113 us; the launch traced here: 112 us
  starting transfers between devices  44 us (39%)
  Pallas kernels  31.2 us (28%)
  waiting for transfers between devices  22 us (19%)
  local copies, waits for them, and re-layouts  10.2 us (9%)
  other arithmetic  3.52 us (3%)
    pallas_call x4, Pallas kernels, down_block(): pl.pallas_call(down_kernel, out_shape=(jax.ShapeDtypeStruct((128, 128), F...  12.2 us
    ppermute x9, starting transfers between devices, along_z(): lax.ppermute(value, BOTH, pairs_of(lambda z, x, y, t, c: (z, x, y, t ^ k,...  11.6 us
    ppermute x5, starting transfers between devices, swap_core(): lax.ppermute(value, BOTH, pairs_of(lambda z, x, y, t, c: (z, x, y, t, c ^...  7.7 us
    ppermute x6, waiting for transfers between devices, first_axis(): lax.ppermute(value, BOTH, pairs_of(lambda z, x, y, t, c: (z, x ^ (0 if c...  7.39 us
    ppermute x1, starting transfers between devices, cross_z(): lax.ppermute(value, BOTH, pairs_of(lambda z, x, y, t, c: (z ^ c, x, y, t,...  7.08 us
    ppermute x6, starting transfers between devices, second_axis(): lax.ppermute(value, BOTH, pairs_of(lambda z, x, y, t, c: (z, x ^ (k if c...  6.9 us
    pallas_call x1, Pallas kernels, cached_attention(): pl.pallas_call(attention_kernel, grid=(rows // per,), out_shape=(wide, wi...  6.37 us
    pallas_call x1, Pallas kernels, base_projection(): pl.pallas_call(base_kernel, grid=(8,), out_shape=jax.ShapeDtypeStruct((gr...  6.09 us
  transfers between devices with their start and end apart: 28, of which 13 were waited for; matrix products, arithmetic and copies ran while one was open for 7% of the time, Pallas kernels for 21%

profile of v2, /device:TPU:1, one launch (start us, length us, event | category | flops | bytes accessed | tf_op | source)
XLA Modules:
  0.0 111.9 jit_solution(1822363631263470784)
XLA Ops:
  1.5 3.3 %collective-permute-start.1 = (bf16[32,1024]{1,0:T(8,128)(2,1)S(1)}, bf16[32,1024]{1,0:T(8,128)(2,1)S(1)}, u32[]{:S(2)}, u32[]{:S(2)}) collective-permute-start(bf16[32,1024]{1,0:T(8,128)(2,1)S(1)} %reshape.76.own_ref), channel_id=1, source_target_pairs={{0,1},{1,0},{2,3},{3,2},{4,5},{5,4},{6,7},{7,6},{8,9},{9,8},{10,11... | collective-permute-start | bytes 196616 | tf_op jit(solution)/shard_map/ppermute | solution.py:27
  5.8 7.1 %collective-permute-start.2 = (bf16[2,32,1024]{2,1,0:T(8,128)(2,1)S(1)}, bf16[2,32,1024]{2,1,0:T(8,128)(2,1)S(1)}, u32[]{:S(2)}, u32[]{:S(2)}) collective-permute-start(bf16[2,32,1024]{2,1,0:T(8,128)(2,1)S(1)} %pad_maximum_fusion.2.p_ref), channel_id=1, source_target_pairs={{0,0},{1,129},{2,2},{3,131},{4,4},{5,133},{6,6},{7,135},{8,8},{9,1... | collective-permute-start | bytes 393224 | tf_op jit(solution)/shard_map/ppermute | solution.py:31
  12.9 2.6 %collective-permute-done.2 = bf16[2,32,1024]{2,1,0:T(8,128)(2,1)S(1)} collective-permute-done((bf16[2,32,1024]{2,1,0:T(8,128)(2,1)S(1)}, bf16[2,32,1024]{2,1,0:T(8,128)(2,1)S(1)}, u32[]{:S(2)}, u32[]{:S(2)}) %collective-permute-start.2) | collective-permute-done | bytes 131104 | tf_op jit(solution)/shard_map/ppermute | solution.py:31
  15.5 2.5 %collective-permute-start.5 = (bf16[2,32,1024]{2,1,0:T(8,128)(2,1)S(1)}, bf16[2,32,1024]{2,1,0:T(8,128)(2,1)S(1)}, u32[]{:S(2)}, u32[]{:S(2)}) collective-permute-start(bf16[2,32,1024]{2,1,0:T(8,128)(2,1)S(1)} %collective-permute-done.2), channel_id=1, source_target_pairs={{0,96},{1,25},{2,98},{3,27},{4,100},{5,29},{6,102},{7,31},{8,104},... | collective-permute-start | bytes 393224 | tf_op jit(solution)/shard_map/ppermute | solution.py:35
  18.7 2.6 %collective-permute-done.5 = bf16[2,32,1024]{2,1,0:T(8,128)(2,1)S(1)} collective-permute-done((bf16[2,32,1024]{2,1,0:T(8,128)(2,1)S(1)}, bf16[2,32,1024]{2,1,0:T(8,128)(2,1)S(1)}, u32[]{:S(2)}, u32[]{:S(2)}) %collective-permute-start.5) | collective-permute-done | bytes 131104 | tf_op jit(solution)/shard_map/ppermute | solution.py:35
  21.4 2.0 %collective-permute-done.4 = bf16[2,32,1024]{2,1,0:T(8,128)(2,1)S(1)} collective-permute-done((bf16[2,32,1024]{2,1,0:T(8,128)(2,1)S(1)}, bf16[2,32,1024]{2,1,0:T(8,128)(2,1)S(1)}, u32[]{:S(2)}, u32[]{:S(2)}) %collective-permute-start.4) | collective-permute-done | bytes 131104 | tf_op jit(solution)/shard_map/ppermute | solution.py:35
  24.7 1.8 %collective-permute-start.13 = (bf16[4,2,32,1024]{3,2,1,0:T(8,128)(2,1)S(1)}, bf16[4,2,32,1024]{3,2,1,0:T(8,128)(2,1)S(1)}, u32[]{:S(2)}, u32[]{:S(2)}) collective-permute-start(bf16[4,2,32,1024]{3,2,1,0:T(8,128)(2,1)S(1)} %pad_maximum_fusion.after_ref.x_ref), channel_id=1, source_target_pairs={{0,24},{1,97},{2,26},{3,99},{4,28},{5,101},{6,30},{7,103},{8,16},{... | collective-permute-start | bytes 1572872 | tf_op jit(solution)/shard_map/ppermute | solution.py:43
  31.3 2.1 %masks.1 = (s32[4,128,128]{2,1,0:T(8,128)}, bf16[512,512]{1,0:T(8,128)(2,1)}, bf16[32,1024]{1,0:T(8,128)(2,1)}) custom-call(s32[16]{0:T(128)} %xor.25.groups_ref, s32[1]{0:T(128)} %bitcast.1.first_ref, s32[32,32,128]{2,1,0:T(8,128)} %broadcast_in_dim.21.ids_ref, bf16[4,64,256]{2,1,0:T(8,128)(2,1)} %up_own_ref.1, bf16[4,64,256]{2,1,0:T(8,128)(2,1)} %copy-done.14, ...), custom_call_target="tpu_custom_call" | custom-call | flops 1000000 | bytes 2000000 | tf_op jit(solution)/shard_map/masks/pallas_call | solution.py:89
  34.1 6.4 %cached.1 = (f32[16,16,128]{2,1,0:T(8,128)}, f32[16,16,128]{2,1,0:T(8,128)}, f32[16,16,128]{2,1,0:T(8,128)}) custom-call(s32[16]{0:T(128)} %lengths_ref.1, bf16[16,16,128]{2,1,0:T(8,128)(2,1)} %reshape.78.q_ref, bf16[16,512,128]{2,1,0:T(8,128)(2,1)} %k_ref.1, bf16[16,512,128]{2,1,0:T(8,128)(2,1)} %v_ref.1, bf16[4,2,32,1024]{3,2,1,0:T(8,128)(2,1)} %copy-done.1), custom_call_target="tpu_custom_call" | custom-call | flops 67108864 | bytes 4194304 | tf_op jit(solution)/shard_map/cached/pallas_call | solution.py:186
  42.1 2.4 %collective-permute-start.7 = (bf16[32,1024]{1,0:T(8,128)(2,1)S(1)}, bf16[32,1024]{1,0:T(8,128)(2,1)S(1)}, u32[]{:S(2)}, u32[]{:S(2)}) collective-permute-start(bf16[32,1024]{1,0:T(8,128)(2,1)S(1)} %copy-done.15), channel_id=1, source_target_pairs={{0,4},{1,5},{2,6},{3,7},{4,0},{5,1},{6,2},{7,3},{8,12},{9,13},{10,... | collective-permute-start | bytes 196616 | tf_op jit(solution)/shard_map/ppermute | solution.py:51
  45.8 3.0 %down.4 = (f32[128,128]{1,0:T(8,128)}, bf16[128,128]{1,0:T(8,128)(2,1)}) custom-call(bf16[4,2,32,1024]{3,2,1,0:T(8,128)(2,1)} %copy-done.1, bf16[4,1024,128]{2,1,0:T(8,128)(2,1)} %own_ref.7, bf16[4,1024,128]{2,1,0:T(8,128)(2,1)} %copy-done, s32[128,128]{1,0:T(8,128)} %get-tuple-element.41.code_ref), custom_call_target="tpu_custom_call" | custom-call | flops 268435456 | bytes 1000000 | tf_op jit(solution)/shard_map/down/pallas_call | solution.py:119
  48.8 3.0 %down.5 = (f32[128,128]{1,0:T(8,128)}, bf16[128,128]{1,0:T(8,128)(2,1)}) custom-call(bf16[4,2,32,1024]{3,2,1,0:T(8,128)(2,1)} %copy-done.11, bf16[4,1024,128]{2,1,0:T(8,128)(2,1)} %own_ref.7, bf16[4,1024,128]{2,1,0:T(8,128)(2,1)} %copy-done, s32[128,128]{1,0:T(8,128)} %get-tuple-element.40.code_ref), custom_call_target="tpu_custom_call" | custom-call | flops 268435456 | bytes 1000000 | tf_op jit(solution)/shard_map/down/pallas_call | solution.py:119
  52.6 3.1 %down.7 = (f32[128,128]{1,0:T(8,128)}, bf16[128,128]{1,0:T(8,128)(2,1)}) custom-call(bf16[4,2,32,1024]{3,2,1,0:T(8,128)(2,1)} %copy-done.10, bf16[4,1024,128]{2,1,0:T(8,128)(2,1)} %own_ref.7, bf16[4,1024,128]{2,1,0:T(8,128)(2,1)} %copy-done, s32[128,128]{1,0:T(8,128)} %get-tuple-element.38.code_ref), custom_call_target="tpu_custom_call" | custom-call | flops 268435456 | bytes 1000000 | tf_op jit(solution)/shard_map/down/pallas_call | solution.py:119
  56.6 3.0 %down.6 = (f32[128,128]{1,0:T(8,128)}, bf16[128,128]{1,0:T(8,128)(2,1)}) custom-call(bf16[4,2,32,1024]{3,2,1,0:T(8,128)(2,1)} %copy-done.12, bf16[4,1024,128]{2,1,0:T(8,128)(2,1)} %own_ref.7, bf16[4,1024,128]{2,1,0:T(8,128)(2,1)} %copy-done, s32[128,128]{1,0:T(8,128)} %get-tuple-element.39.code_ref, f32[16,16,128]{2,1,0:T(8,128)} %get-tuple-element.24.rest_0_.top_ref, ...), custom_call_target="tpu_custom_call" | custom-call | flops 268435456 | bytes 1000000 | tf_op jit(solution)/shard_map/down/pallas_call | solution.py:119
  60.5 2.1 %collective-permute-start.16 = (bf16[128,128]{1,0:T(8,128)(2,1)S(1)}, bf16[128,128]{1,0:T(8,128)(2,1)S(1)}, u32[]{:S(2)}, u32[]{:S(2)}) collective-permute-start(bf16[128,128]{1,0:T(8,128)(2,1)S(1)} %get-tuple-element.46), channel_id=1, source_target_pairs={{0,6},{1,7},{2,4},{3,5},{4,2},{5,3},{6,0},{7,1},{8,14},{9,15},{10,... | collective-permute-start | bytes 98312 | tf_op jit(solution)/shard_map/ppermute | solution.py:51
  70.8 3.1 %collective-permute-done.19.r3 = bf16[128,128]{1,0:T(8,128)(2,1)S(1)} collective-permute-done((bf16[128,128]{1,0:T(8,128)(2,1)S(1)}, bf16[128,128]{1,0:T(8,128)(2,1)S(1)}, u32[]{:S(2)}, u32[]{:S(2)}) %collective-permute-start.19) | collective-permute-done | bytes 32800 | tf_op jit(solution)/shard_map/ppermute | solution.py:51
  74.5 2.3 %up.1 = (bf16[128,512]{1,0:T(8,128)(2,1)}, bf16[128,512]{1,0:T(8,128)(2,1)}, bf16[128,512]{1,0:T(8,128)(2,1)}, bf16[128,512]{1,0:T(8,128)(2,1)}) custom-call(s32[1]{0:T(128)} %bitcast.12.t_ref, bf16[128,128]{1,0:T(8,128)(2,1)} %copy-done.19, bf16[128,128]{1,0:T(8,128)(2,1)} %copy-done.25, bf16[128,128]{1,0:T(8,128)(2,1)} %copy-done.26, ...), custom_call_target="tpu_custom_call" | custom-call | flops 268435456 | bytes 2000000 | tf_op jit(solution)/shard_map/up/pallas_call | solution.py:149
  76.8 2.3 %collective-permute-start.22 = (bf16[128,512]{1,0:T(8,128)(2,1)}, bf16[128,512]{1,0:T(8,128)(2,1)S(1)}, u32[]{:S(2)}, u32[]{:S(2)}) collective-permute-start(bf16[128,512]{1,0:T(8,128)(2,1)} %get-tuple-element.35), channel_id=1, source_target_pairs={{0,16},{1,65},{2,18},{3,67},{4,20},{5,69},{6,22},{7,71},{8,24},{9,... | collective-permute-start | bytes 393224 | tf_op jit(solution)/shard_map/ppermute | solution.py:43
  80.2 2.5 %collective-permute-done.22 = bf16[128,512]{1,0:T(8,128)(2,1)S(1)} collective-permute-done((bf16[128,512]{1,0:T(8,128)(2,1)}, bf16[128,512]{1,0:T(8,128)(2,1)S(1)}, u32[]{:S(2)}, u32[]{:S(2)}) %collective-permute-start.22) | collective-permute-done | bytes 131104 | tf_op jit(solution)/shard_map/ppermute | solution.py:43
  82.7 2.0 %collective-permute-done.21 = bf16[128,512]{1,0:T(8,128)(2,1)S(1)} collective-permute-done((bf16[128,512]{1,0:T(8,128)(2,1)}, bf16[128,512]{1,0:T(8,128)(2,1)S(1)}, u32[]{:S(2)}, u32[]{:S(2)}) %collective-permute-start.21) | collective-permute-done | bytes 131104 | tf_op jit(solution)/shard_map/ppermute | solution.py:43
  91.3 4.1 %collective-permute-start.26 = (bf16[32,256]{1,0:T(8,128)(2,1)S(1)}, bf16[32,256]{1,0:T(8,128)(2,1)S(1)}, u32[]{:S(2)}, u32[]{:S(2)}) collective-permute-start(bf16[32,256]{1,0:T(8,128)(2,1)S(1)} %slice.49), channel_id=1, source_target_pairs={{0,1},{1,0},{2,3},{3,2},{4,5},{5,4},{6,7},{7,6},{8,9},{9,8},{10,11... | collective-permute-start | bytes 49160 | tf_op jit(solution)/shard_map/ppermute | solution.py:27
  96.9 4.8 %collective-permute-start.27 = (bf16[32,256]{1,0:T(8,128)(2,1)S(1)}, bf16[32,256]{1,0:T(8,128)(2,1)S(1)}, u32[]{:S(2)}, u32[]{:S(2)}) collective-permute-start(bf16[32,256]{1,0:T(8,128)(2,1)S(1)} %get-tuple-element.48), channel_id=1, source_target_pairs={{0,128},{1,129},{2,130},{3,131},{4,132},{5,133},{6,134},{7,135},{8... | collective-permute-start | bytes 49160 | tf_op jit(solution)/shard_map/ppermute | solution.py:55
  103.0 6.1 %base.1.base_ref = f32[32,256]{1,0:T(8,128)} custom-call(s32[1]{0:T(128)} %bitcast.j_ref, bf16[32,1024]{1,0:T(8,128)(2,1)} %get-tuple-element.20.s0, bf16[32,1024]{1,0:T(8,128)(2,1)} %copy-done.2, bf16[32,1024]{1,0:T(8,128)(2,1)} %copy-done.4, bf16[32,1024]{1,0:T(8,128)(2,1)} %copy-done.6, bf16[2,32,1024]{2,1,0:T(8,128)(2,1)} %copy-done.9, ...), custom_call_target="tpu_custom_call" | custom-call | flops 134217728 | bytes 4194304 | tf_op jit(solution)/shard_map/base/pallas_call | solution.py:220
  109.7 2.2 %merge.1 = (bf16[16,2,256]{2,1,0:T(2,128)(2,1)}, bf16[16,2,1024]{2,1,0:T(2,128)(2,1)}) custom-call(f32[32,256]{1,0:T(8,128)} %base.1.base_ref, bf16[32,256]{1,0:T(8,128)(2,1)} %get-tuple-element.49.kept_ref, bf16[32,256]{1,0:T(8,128)(2,1)} %copy-done.23, f32[32,128]{1,0:T(8,128)} %get-tuple-element.53.cos_ref, f32[32,128]{1,0:T(8,128)} %get-tuple-element.54.sin_ref, ...), custom_call_target="tpu_custom_call" | custom-call | flops 2000000 | bytes 1000000 | tf_op jit(solution)/shard_map/merge/pallas_call | solution.py:276
  (124 shorter events, 34.3 us)
Async XLA Ops:
  1.5 4.2 %collective-permute-start.1 = (bf16[32,1024]{1,0:T(8,128)(2,1)S(1)}, bf16[32,1024]{1,0:T(8,128)(2,1)S(1)}, u32[]{:S(2)}, u32[]{:S(2)}) collective-permute-start(bf16[32,1024]{1,0:T(8,128)(2,1)S(1)} %reshape.76.own_ref), channel_id=1, source_target_pairs={{0,1},{1,0},{2,3},{3,2},{4,5},{5,4},{6,7},{7,6},{8,9},{9,8},{10,11... | collective-permute-start | bytes 196616 | tf_op jit(solution)/shard_map/ppermute | solution.py:27
  4.8 39.7 %collective-permute-start.10 = (bf16[4,1024,128]{2,1,0:T(8,128)(2,1)}, bf16[4,1024,128]{2,1,0:T(8,128)(2,1)S(1)}, u32[]{:S(2)}, u32[]{:S(2)}) collective-permute-start(bf16[4,1024,128]{2,1,0:T(8,128)(2,1)} %own_ref.7), channel_id=1, source_target_pairs={{0,1},{1,0},{2,3},{3,2},{4,5},{5,4},{6,7},{7,6},{8,9},{9,8},{10,11... | collective-permute-start | bytes 3145736 | tf_op jit(solution)/shard_map/ppermute | solution.py:27
  5.8 9.7 %collective-permute-start.2 = (bf16[2,32,1024]{2,1,0:T(8,128)(2,1)S(1)}, bf16[2,32,1024]{2,1,0:T(8,128)(2,1)S(1)}, u32[]{:S(2)}, u32[]{:S(2)}) collective-permute-start(bf16[2,32,1024]{2,1,0:T(8,128)(2,1)S(1)} %pad_maximum_fusion.2.p_ref), channel_id=1, source_target_pairs={{0,0},{1,129},{2,2},{3,131},{4,4},{5,133},{6,6},{7,135},{8,8},{9,1... | collective-permute-start | bytes 393224 | tf_op jit(solution)/shard_map/ppermute | solution.py:31
  15.5 5.9 %collective-permute-start.5 = (bf16[2,32,1024]{2,1,0:T(8,128)(2,1)S(1)}, bf16[2,32,1024]{2,1,0:T(8,128)(2,1)S(1)}, u32[]{:S(2)}, u32[]{:S(2)}) collective-permute-start(bf16[2,32,1024]{2,1,0:T(8,128)(2,1)S(1)} %collective-permute-done.2), channel_id=1, source_target_pairs={{0,96},{1,25},{2,98},{3,27},{4,100},{5,29},{6,102},{7,31},{8,104},... | collective-permute-start | bytes 393224 | tf_op jit(solution)/shard_map/ppermute | solution.py:35
  18.0 5.3 %collective-permute-start.4 = (bf16[2,32,1024]{2,1,0:T(8,128)(2,1)S(1)}, bf16[2,32,1024]{2,1,0:T(8,128)(2,1)S(1)}, u32[]{:S(2)}, u32[]{:S(2)}) collective-permute-start(bf16[2,32,1024]{2,1,0:T(8,128)(2,1)S(1)} %collective-permute-done.2), channel_id=1, source_target_pairs={{0,64},{1,17},{2,66},{3,19},{4,68},{5,21},{6,70},{7,23},{8,72},{9,... | collective-permute-start | bytes 393224 | tf_op jit(solution)/shard_map/ppermute | solution.py:35
  18.4 5.0 %collective-permute-start.3 = (bf16[2,32,1024]{2,1,0:T(8,128)(2,1)S(1)}, bf16[2,32,1024]{2,1,0:T(8,128)(2,1)S(1)}, u32[]{:S(2)}, u32[]{:S(2)}) collective-permute-start(bf16[2,32,1024]{2,1,0:T(8,128)(2,1)S(1)} %collective-permute-done.2), channel_id=1, source_target_pairs={{0,32},{1,9},{2,34},{3,11},{4,36},{5,13},{6,38},{7,15},{8,40},{9,1... | collective-permute-start | bytes 393224 | tf_op jit(solution)/shard_map/ppermute | solution.py:35
  18.7 11.6 %collective-permute-start = (bf16[4,64,256]{2,1,0:T(8,128)(2,1)}, bf16[4,64,256]{2,1,0:T(8,128)(2,1)S(1)}, u32[]{:S(2)}, u32[]{:S(2)}) collective-permute-start(bf16[4,64,256]{2,1,0:T(8,128)(2,1)} %up_own_ref.1), channel_id=1, source_target_pairs={{0,1},{1,0},{2,3},{3,2},{4,5},{5,4},{6,7},{7,6},{8,9},{9,8},{10,11... | collective-permute-start | bytes 393224 | tf_op jit(solution)/shard_map/ppermute | solution.py:27
  23.4 18.7 %collective-permute-start.11 = (bf16[4,2,32,1024]{3,2,1,0:T(8,128)(2,1)S(1)}, bf16[4,2,32,1024]{3,2,1,0:T(8,128)(2,1)S(1)}, u32[]{:S(2)}, u32[]{:S(2)}) collective-permute-start(bf16[4,2,32,1024]{3,2,1,0:T(8,128)(2,1)S(1)} %pad_maximum_fusion.after_ref.x_ref), channel_id=1, source_target_pairs={{0,8},{1,33},{2,10},{3,35},{4,12},{5,37},{6,14},{7,39},{8,0},{9,41... | collective-permute-start | bytes 1572872 | tf_op jit(solution)/shard_map/ppermute | solution.py:43
  24.7 27.1 %collective-permute-start.13 = (bf16[4,2,32,1024]{3,2,1,0:T(8,128)(2,1)S(1)}, bf16[4,2,32,1024]{3,2,1,0:T(8,128)(2,1)S(1)}, u32[]{:S(2)}, u32[]{:S(2)}) collective-permute-start(bf16[4,2,32,1024]{3,2,1,0:T(8,128)(2,1)S(1)} %pad_maximum_fusion.after_ref.x_ref), channel_id=1, source_target_pairs={{0,24},{1,97},{2,26},{3,99},{4,28},{5,101},{6,30},{7,103},{8,16},{... | collective-permute-start | bytes 1572872 | tf_op jit(solution)/shard_map/ppermute | solution.py:43
  26.6 29.2 %collective-permute-start.12 = (bf16[4,2,32,1024]{3,2,1,0:T(8,128)(2,1)S(1)}, bf16[4,2,32,1024]{3,2,1,0:T(8,128)(2,1)S(1)}, u32[]{:S(2)}, u32[]{:S(2)}) collective-permute-start(bf16[4,2,32,1024]{3,2,1,0:T(8,128)(2,1)S(1)} %pad_maximum_fusion.after_ref.x_ref), channel_id=1, source_target_pairs={{0,16},{1,65},{2,18},{3,67},{4,20},{5,69},{6,22},{7,71},{8,24},{9,... | collective-permute-start | bytes 1572872 | tf_op jit(solution)/shard_map/ppermute | solution.py:43
  33.5 22.3 %collective-permute-start.6 = (bf16[32,1024]{1,0:T(8,128)(2,1)}, bf16[32,1024]{1,0:T(8,128)(2,1)S(1)}, u32[]{:S(2)}, u32[]{:S(2)}) collective-permute-start(bf16[32,1024]{1,0:T(8,128)(2,1)} %get-tuple-element.20.s0), channel_id=1, source_target_pairs={{0,2},{1,3},{2,0},{3,1},{4,6},{5,7},{6,4},{7,5},{8,10},{9,11},{10,... | collective-permute-start | bytes 196616 | tf_op jit(solution)/shard_map/ppermute | solution.py:51
  42.1 13.6 %collective-permute-start.7 = (bf16[32,1024]{1,0:T(8,128)(2,1)S(1)}, bf16[32,1024]{1,0:T(8,128)(2,1)S(1)}, u32[]{:S(2)}, u32[]{:S(2)}) collective-permute-start(bf16[32,1024]{1,0:T(8,128)(2,1)S(1)} %copy-done.15), channel_id=1, source_target_pairs={{0,4},{1,5},{2,6},{3,7},{4,0},{5,1},{6,2},{7,3},{8,12},{9,13},{10,... | collective-permute-start | bytes 196616 | tf_op jit(solution)/shard_map/ppermute | solution.py:51
  44.5 11.2 %collective-permute-start.8 = (bf16[32,1024]{1,0:T(8,128)(2,1)S(1)}, bf16[32,1024]{1,0:T(8,128)(2,1)S(1)}, u32[]{:S(2)}, u32[]{:S(2)}) collective-permute-start(bf16[32,1024]{1,0:T(8,128)(2,1)S(1)} %copy-done.15), channel_id=1, source_target_pairs={{0,6},{1,7},{2,4},{3,5},{4,2},{5,3},{6,0},{7,1},{8,14},{9,15},{10,... | collective-permute-start | bytes 196616 | tf_op jit(solution)/shard_map/ppermute | solution.py:51
  60.5 4.7 %collective-permute-start.16 = (bf16[128,128]{1,0:T(8,128)(2,1)S(1)}, bf16[128,128]{1,0:T(8,128)(2,1)S(1)}, u32[]{:S(2)}, u32[]{:S(2)}) collective-permute-start(bf16[128,128]{1,0:T(8,128)(2,1)S(1)} %get-tuple-element.46), channel_id=1, source_target_pairs={{0,6},{1,7},{2,4},{3,5},{4,2},{5,3},{6,0},{7,1},{8,14},{9,15},{10,... | collective-permute-start | bytes 98312 | tf_op jit(solution)/shard_map/ppermute | solution.py:51
  67.1 3.7 %collective-permute-start.18 = (bf16[128,128]{1,0:T(8,128)(2,1)S(1)}, bf16[128,128]{1,0:T(8,128)(2,1)S(1)}, u32[]{:S(2)}, u32[]{:S(2)}) collective-permute-start(bf16[128,128]{1,0:T(8,128)(2,1)S(1)} %fusion.7.r0), channel_id=1, source_target_pairs={{0,4},{1,5},{2,6},{3,7},{4,0},{5,1},{6,2},{7,3},{8,12},{9,13},{10,... | collective-permute-start | bytes 98312 | tf_op jit(solution)/shard_map/ppermute | solution.py:51
  68.9 5.0 %collective-permute-start.19 = (bf16[128,128]{1,0:T(8,128)(2,1)S(1)}, bf16[128,128]{1,0:T(8,128)(2,1)S(1)}, u32[]{:S(2)}, u32[]{:S(2)}) collective-permute-start(bf16[128,128]{1,0:T(8,128)(2,1)S(1)} %fusion.7.r0), channel_id=1, source_target_pairs={{0,6},{1,7},{2,4},{3,5},{4,2},{5,3},{6,0},{7,1},{8,14},{9,15},{10,... | collective-permute-start | bytes 98312 | tf_op jit(solution)/shard_map/ppermute | solution.py:51
  76.8 5.8 %collective-permute-start.22 = (bf16[128,512]{1,0:T(8,128)(2,1)}, bf16[128,512]{1,0:T(8,128)(2,1)S(1)}, u32[]{:S(2)}, u32[]{:S(2)}) collective-permute-start(bf16[128,512]{1,0:T(8,128)(2,1)} %get-tuple-element.35), channel_id=1, source_target_pairs={{0,16},{1,65},{2,18},{3,67},{4,20},{5,69},{6,22},{7,71},{8,24},{9,... | collective-permute-start | bytes 393224 | tf_op jit(solution)/shard_map/ppermute | solution.py:43
  79.1 5.5 %collective-permute-start.21 = (bf16[128,512]{1,0:T(8,128)(2,1)}, bf16[128,512]{1,0:T(8,128)(2,1)S(1)}, u32[]{:S(2)}, u32[]{:S(2)}) collective-permute-start(bf16[128,512]{1,0:T(8,128)(2,1)} %get-tuple-element.34), channel_id=1, source_target_pairs={{0,24},{1,97},{2,26},{3,99},{4,28},{5,101},{6,30},{7,103},{8,16},{... | collective-permute-start | bytes 393224 | tf_op jit(solution)/shard_map/ppermute | solution.py:43
  80.0 4.7 %collective-permute-start.20 = (bf16[128,512]{1,0:T(8,128)(2,1)}, bf16[128,512]{1,0:T(8,128)(2,1)S(1)}, u32[]{:S(2)}, u32[]{:S(2)}) collective-permute-start(bf16[128,512]{1,0:T(8,128)(2,1)} %get-tuple-element.33), channel_id=1, source_target_pairs={{0,8},{1,33},{2,10},{3,35},{4,12},{5,37},{6,14},{7,39},{8,0},{9,41... | collective-permute-start | bytes 393224 | tf_op jit(solution)/shard_map/ppermute | solution.py:43
  85.6 4.4 %collective-permute-start.25 = (bf16[32,512]{1,0:T(8,128)(2,1)S(1)}, bf16[32,512]{1,0:T(8,128)(2,1)S(1)}, u32[]{:S(2)}, u32[]{:S(2)}) collective-permute-start(bf16[32,512]{1,0:T(8,128)(2,1)S(1)} %get-tuple-element.43), channel_id=1, source_target_pairs={{0,64},{1,17},{2,66},{3,19},{4,68},{5,21},{6,70},{7,23},{8,72},{9,... | collective-permute-start | bytes 98312 | tf_op jit(solution)/shard_map/ppermute | solution.py:35
  87.3 4.0 %collective-permute-start.24 = (bf16[32,512]{1,0:T(8,128)(2,1)S(1)}, bf16[32,512]{1,0:T(8,128)(2,1)S(1)}, u32[]{:S(2)}, u32[]{:S(2)}) collective-permute-start(bf16[32,512]{1,0:T(8,128)(2,1)S(1)} %get-tuple-element.44), channel_id=1, source_target_pairs={{0,96},{1,25},{2,98},{3,27},{4,100},{5,29},{6,102},{7,31},{8,104},... | collective-permute-start | bytes 98312 | tf_op jit(solution)/shard_map/ppermute | solution.py:35
  91.3 5.0 %collective-permute-start.26 = (bf16[32,256]{1,0:T(8,128)(2,1)S(1)}, bf16[32,256]{1,0:T(8,128)(2,1)S(1)}, u32[]{:S(2)}, u32[]{:S(2)}) collective-permute-start(bf16[32,256]{1,0:T(8,128)(2,1)S(1)} %slice.49), channel_id=1, source_target_pairs={{0,1},{1,0},{2,3},{3,2},{4,5},{5,4},{6,7},{7,6},{8,9},{9,8},{10,11... | collective-permute-start | bytes 49160 | tf_op jit(solution)/shard_map/ppermute | solution.py:27
  95.5 6.9 %collective-permute-start.9 = (bf16[3,32,1024]{2,1,0:T(8,128)(2,1)S(1)}, bf16[3,32,1024]{2,1,0:T(8,128)(2,1)S(1)}, u32[]{:S(2)}, u32[]{:S(2)}) collective-permute-start(bf16[3,32,1024]{2,1,0:T(8,128)(2,1)S(1)} %pad_maximum_fusion.1), channel_id=1, source_target_pairs={{0,1},{1,0},{2,3},{3,2},{4,5},{5,4},{6,7},{7,6},{8,9},{9,8},{10,11... | collective-permute-start | bytes 589832 | tf_op jit(solution)/shard_map/ppermute | solution.py:27
  96.9 12.2 %collective-permute-start.27 = (bf16[32,256]{1,0:T(8,128)(2,1)S(1)}, bf16[32,256]{1,0:T(8,128)(2,1)S(1)}, u32[]{:S(2)}, u32[]{:S(2)}) collective-permute-start(bf16[32,256]{1,0:T(8,128)(2,1)S(1)} %get-tuple-element.48), channel_id=1, source_target_pairs={{0,128},{1,129},{2,130},{3,131},{4,132},{5,133},{6,134},{7,135},{8... | collective-permute-start | bytes 49160 | tf_op jit(solution)/shard_map/ppermute | solution.py:55
  (32 other events, 298.4 us)

commit v3 on v2

v3 whole, which is shorter than its diff:
```python
import functools
import math

import jax
import jax.numpy as jnp
from jax import lax
from jax.experimental import pallas as pl
from jax.experimental.pallas import tpu as pltpu
from jax.sharding import PartitionSpec as P

HEAD_SIZE = 128
F32 = jnp.float32
BF16 = jnp.bfloat16
BOTH = ("dp", "tensor")


def pairs_of(move):
    pairs = []
    for d in range(32):
        for j in range(8):
            z, x, y, t, c = d // 16, d // 4 % 4, d % 4, j // 2, j % 2
            z, x, y, t, c = move(z, x, y, t, c)
            pairs.append((d * 8 + j, (z * 16 + x * 4 + y) * 8 + t * 2 + c))
    return pairs


def swap_core(value):
    return lax.ppermute(value, BOTH, pairs_of(lambda z, x, y, t, c: (z, x, y, t, c ^ 1)))


def cross_z(value):
    return lax.ppermute(value, BOTH, pairs_of(lambda z, x, y, t, c: (z ^ c, x, y, t, c)))


def first_axis(value, k):
    return lax.ppermute(
        value,
        BOTH,
        pairs_of(lambda z, x, y, t, c: (z, x ^ (0 if c else k), y ^ (k if c else 0), t, c)),
    )


def second_axis(value, k):
    return lax.ppermute(
        value,
        BOTH,
        pairs_of(lambda z, x, y, t, c: (z, x ^ (k if c else 0), y ^ (0 if c else k), t, c)),
    )


def along_x(value, k):
    return lax.ppermute(value, BOTH, pairs_of(lambda z, x, y, t, c: (z, x ^ (0 if c else k), y ^ (k if c else 0), t, c)))


def along_y(value, k):
    return lax.ppermute(value, BOTH, pairs_of(lambda z, x, y, t, c: (z, x ^ (k if c else 0), y ^ (0 if c else k), t, c)))


def along_z(value, k):
    return lax.ppermute(value, BOTH, pairs_of(lambda z, x, y, t, c: (z, x, y, t ^ k, c)))


def swap_z(value):
    return lax.ppermute(value, BOTH, pairs_of(lambda z, x, y, t, c: (z ^ 1, x, y, t, c)))


def anywhere():
    return pl.BlockSpec(memory_space=pl.ANY)


def hbm():
    return pl.BlockSpec(memory_space=pltpu.HBM)


def vmem():
    return pl.BlockSpec(memory_space=pltpu.VMEM)


def smem():
    return pl.BlockSpec(memory_space=pltpu.SMEM)


def limit(mebibytes):
    return pltpu.CompilerParams(vmem_limit_bytes=mebibytes << 20)


def small(name, kernel, out_shape, in_specs, args, mebibytes=2, scratch=()):
    many = isinstance(out_shape, (list, tuple))
    return pl.pallas_call(
        kernel,
        out_shape=out_shape,
        in_specs=in_specs,
        out_specs=[vmem()] * len(out_shape) if many else vmem(),
        scratch_shapes=scratch,
        name=name,
        compiler_params=limit(mebibytes),
        cost_estimate=pl.CostEstimate(flops=100_000, bytes_accessed=200_000, transcendentals=0),
    )(*args)


def stack_kernel(*refs):
    for n in range(refs[-1].shape[0]):
        refs[-1][n] = refs[n][...]


def stack(*parts, after=None):
    shape = jax.ShapeDtypeStruct((len(parts), *parts[0].shape), parts[0].dtype)
    specs = [vmem()] * len(parts)
    if after is not None:
        parts, specs = (*parts, after), [*specs, anywhere()]
    return small("stack", stack_kernel, shape, specs, parts)


def line_kernel(a_ref, b_ref, c_ref, d_ref, low_ref, high_ref):
    low_ref[0] = a_ref[...]
    low_ref[1] = b_ref[...]
    high_ref[0] = c_ref[...]
    high_ref[1] = d_ref[...]


def line_halves(*parts):
    shape = jax.ShapeDtypeStruct((2, *parts[0].shape), parts[0].dtype)
    return small("line", line_kernel, (shape, shape), [vmem()] * 4, parts, 3)


def pack_kernel(n_ref, *refs):
    out_ref = refs[-1]
    for m in range(4):
        out_ref[2 * m : 2 * m + 2] = refs[m][...]
        out_ref[8 + m] = n_ref[0] if m == 0 else refs[3 + m][1]


def pack(chunks, *parts):
    shape = jax.ShapeDtypeStruct((12, *parts[0].shape[1:]), parts[0].dtype)
    return small("pack", pack_kernel, shape, [vmem()] * 8, (chunks, *parts))


def query_kernel(lengths_ref, q_ref, after_ref, out_ref, bias_ref):
    out_ref[...] = q_ref[...]
    spot = lax.broadcasted_iota(jnp.int32, (1, bias_ref.shape[1]), 1)
    for r in range(bias_ref.shape[0]):
        bias_ref[r : r + 1, :] = jnp.where(spot < lengths_ref[r], 0.0, -jnp.inf)


def ready_queries(lengths, q, context, after):
    shapes = (
        jax.ShapeDtypeStruct(q.shape, q.dtype),
        jax.ShapeDtypeStruct((q.shape[0], context), F32),
    )
    return small("query", query_kernel, shapes, [smem(), vmem(), vmem()], (lengths, q, after))


def chunk_kernel(own_ref, after_ref, *out_refs):
    for h, out_ref in enumerate(out_refs):
        for i in range(4):
            at = h * 512 + i * 128
            out_ref[0, 32 * i : 32 * i + 32, :] = own_ref[:, at : at + 128]


def make_chunks(own, after):
    shapes = (jax.ShapeDtypeStruct((1, 128, 128), BF16),) * 2
    return small("chunks", chunk_kernel, shapes, [vmem(), vmem()], (own, after))


def wide_kernel(up_ref, after_ref, wide_ref):
    wide_ref[...] = jnp.zeros_like(wide_ref)
    for a in range(up_ref.shape[0]):
        wide_ref[128 * a : 128 * a + 64, :128] = up_ref[a, :, :128]
        wide_ref[128 * a + 64 : 128 * a + 128, 128:] = up_ref[a, :, 128:]


def widen(up, after):
    shape = jax.ShapeDtypeStruct((up.shape[0] * 128, 256), BF16)
    return small("widen", wide_kernel, shape, [vmem(), vmem()], (up, after))


def code_kernel(groups_ref, first_ref, ids_ref, after_ref, out_ref, held):
    rows = ids_ref.shape[1]
    place = lax.broadcasted_iota(jnp.int32, (rows, 2 * rows), 1) // 2
    twice = (place == lax.broadcasted_iota(jnp.int32, (rows, 2 * rows), 0)).astype(BF16)
    ids = ids_ref[...].astype(F32).astype(BF16)
    held[...] = jnp.dot(ids, twice, preferred_element_type=F32) - first_ref[0].astype(F32)
    for n in range(out_ref.shape[0]):
        picked = [held[pl.ds(groups_ref[4 * n + k], 1), :] for k in range(4)]
        out_ref[n : n + 1, :] = jnp.concatenate(picked, 1)


def make_codes(groups, first, ids, after):
    return pl.pallas_call(
        code_kernel,
        out_shape=jax.ShapeDtypeStruct((8, 128), F32),
        in_specs=[smem(), smem(), vmem(), vmem()],
        out_specs=vmem(),
        scratch_shapes=[pltpu.VMEM((ids.shape[0], 2 * ids.shape[1]), F32)],
        name="codes",
        compiler_params=limit(1),
        cost_estimate=pl.CostEstimate(flops=100_000, bytes_accessed=100_000, transcendentals=0),
    )(groups, first, ids, after)


def column(codes_ref, n):
    return jnp.broadcast_to(codes_ref[n : n + 1, :], (128, 128)).T


def down_kernel(block, low_ref, high_ref, own_ref, other_ref, codes_ref, *rest):
    out_ref = rest[-1]
    half = low_ref.shape[0] * low_ref.shape[2]
    sides = [
        jnp.concatenate([ref[:, n].reshape(half, ref.shape[3]) for ref in (low_ref, high_ref)], 0)
        for n in range(2)
    ]
    code = column(codes_ref, block)
    total = jnp.zeros(out_ref.shape, F32)
    for a in range(own_ref.shape[0]):
        product = jnp.dot(sides[0], own_ref[a], preferred_element_type=F32)
        product = product + jnp.dot(sides[1], other_ref[a], preferred_element_type=F32)
        total = jnp.where(code == a, product, total)
    out_ref[...] = total.astype(BF16)


def down_block(block, halves, own, other, codes, after=()):
    return pl.pallas_call(
        functools.partial(down_kernel, block),
        out_shape=jax.ShapeDtypeStruct((128, 128), BF16),
        in_specs=[vmem()] * 5 + [anywhere()] * len(after),
        out_specs=vmem(),
        name="down",
        compiler_params=limit(6),
        cost_estimate=pl.CostEstimate(
            flops=2 * 128 * 2048 * 512, bytes_accessed=1_000_000, transcendentals=0
        ),
    )(*halves, own, other, codes, *after)


def up_kernel(t_ref, r0, r1, r2, r3, other_ref, codes_ref, wide_ref, d0, d1, d2, d3, held):
    t = t_ref[0]
    outs = (d0, d1, d2, d3)
    for m, ref in enumerate((r0, r1, r2, r3)):
        held[m] = ref[0]

    def grown(low, code):
        low = low.astype(F32)
        spread = jnp.concatenate(
            [jnp.where(code == a, low, 0.0).astype(BF16) for a in range(wide_ref.shape[0] // 128)],
            1,
        )
        return jnp.dot(spread, wide_ref[...], preferred_element_type=F32).astype(BF16)

    for k2 in range(4):
        block = grown(held[jnp.bitwise_xor(t, k2)], column(codes_ref, k2))
        outs[k2][:, 0] = block.reshape(4, 32, 256)
        block = grown(other_ref[2 * jnp.bitwise_xor(t, k2)], column(codes_ref, 4 + k2))
        for k1 in range(4):
            outs[k1][k2, 1] = block[32 * k1 : 32 * k1 + 32]


def up_blocks(t, slots, others, codes, wide):
    return pl.pallas_call(
        up_kernel,
        out_shape=[jax.ShapeDtypeStruct((4, 2, 32, 256), BF16)] * 4,
        in_specs=[smem()] + [vmem()] * 7,
        out_specs=[vmem()] * 4,
        scratch_shapes=[pltpu.VMEM((4, 128, 128), BF16)],
        name="up",
        compiler_params=limit(4),
        cost_estimate=pl.CostEstimate(
            flops=2 * 1024 * 512 * 256, bytes_accessed=2_000_000, transcendentals=0
        ),
    )(t, *slots, others, codes, wide)


def cached_attention(queries, bias, k_cache, value_cache):
    scores = jnp.einsum("rqd,rjd->rqj", queries, k_cache, preferred_element_type=F32)
    scores = scores * (1.0 / math.sqrt(HEAD_SIZE)) + bias[:, None, :]
    top = jnp.max(scores, -1, keepdims=True)
    weight = jnp.exp(scores - top)
    total = jnp.sum(weight, -1, keepdims=True)
    gathered = jnp.einsum(
        "rqj,rjd->rqd", weight.astype(BF16), value_cache, preferred_element_type=F32
    )
    wide = lambda x: jnp.broadcast_to(x, gathered.shape)
    return wide(top), wide(total), gathered


def row_kernel(j_ref, n0, n1, r1, r2, r3, g1, g2, g3, others_ref, out_ref, held):
    own = ((n0, n1), (r1, g1), (r2, g2), (r3, g3))
    for m in range(4):
        for h in range(2):
            held[2 * m, h] = own[m][h][0 if m == 0 else 1]
            held[2 * m + 1, h] = others_ref[2 * m + 1 if h else 8 + m]
    for n in range(8):
        for h in range(2):
            chunk = held[jnp.bitwise_xor(j_ref[0], n), h]
            for i in range(4):
                at = n * 1024 + h * 512 + i * 128
                out_ref[:, at : at + 128] = chunk[32 * i : 32 * i + 32, :]


def whole_rows(j, chunks, scattered, gathered, others):
    return pl.pallas_call(
        row_kernel,
        out_shape=jax.ShapeDtypeStruct((32, 8192), BF16),
        in_specs=[smem()] + [vmem()] * 9,
        out_specs=vmem(),
        scratch_shapes=[pltpu.VMEM((8, 2, 128, 128), BF16)],
        name="rows",
        compiler_params=limit(3),
        cost_estimate=pl.CostEstimate(flops=0, bytes_accessed=1_000_000, transcendentals=0),
    )(j, *chunks, *scattered, *gathered, others)


def split_kernel(c_ref, home_ref, after_ref, kept_ref, sent_ref):
    kept_ref[...] = home_ref[c_ref[0]]
    sent_ref[...] = home_ref[1 - c_ref[0]]


def final_kernel(
    base_ref, kept_ref, came_ref, cos_ref, sin_ref, q_ref, top_ref, total_ref, sum_ref,
    new_ref, out_ref, held, result,
):
    rows, queries, _ = q_ref.shape
    heads = queries // 2
    update = kept_ref[...].astype(F32) + came_ref[...].astype(F32)
    projected = base_ref[...] + update
    key = projected[:, :HEAD_SIZE]
    turned = pltpu.roll(key, HEAD_SIZE // 2, 1)
    key = key * cos_ref[...] + turned * sin_ref[...]
    fresh = jnp.concatenate([key, projected[:, HEAD_SIZE:]], 1).astype(BF16)
    held[0] = fresh[:, :HEAD_SIZE].astype(F32)
    held[1] = fresh[:, HEAD_SIZE:].astype(F32)
    q = q_ref[...].astype(F32)
    scale = 1.0 / math.sqrt(HEAD_SIZE)
    keys = [held[0, pl.ds(s, rows, stride=2), :] for s in range(2)]
    values = [held[1, pl.ds(s, rows, stride=2), :] for s in range(2)]
    scores = [jnp.sum(q * k[:, None, :], -1, keepdims=True) * scale for k in keys]
    second = lax.broadcasted_iota(jnp.int32, scores[1].shape, 1) >= heads
    scores[1] = jnp.where(second, scores[1], -jnp.inf)
    top = top_ref[...]
    highest = jnp.maximum(top, jnp.maximum(scores[0], scores[1]))
    old = jnp.exp(top - highest)
    new = [jnp.exp(s - highest) for s in scores]
    total = total_ref[...] * old + new[0] + new[1]
    mixed = sum_ref[...] * old + new[0] * values[0][:, None, :] + new[1] * values[1][:, None, :]
    result[...] = (mixed / total).reshape(rows * queries, HEAD_SIZE)
    new_ref[:, :, :HEAD_SIZE] = jnp.stack(keys, 1).astype(BF16)
    new_ref[:, :, HEAD_SIZE:] = jnp.stack(values, 1).astype(BF16)
    for g in range(heads):
        both = [result[pl.ds(s * heads + g, rows, stride=queries), :] for s in range(2)]
        out_ref[:, :, HEAD_SIZE * g : HEAD_SIZE * (g + 1)] = jnp.stack(both, 1).astype(BF16)


def final_merge(base, kept, came, cosine, sine, q, top, total, gathered):
    rows, queries, _ = q.shape
    group = 2 * rows
    return pl.pallas_call(
        final_kernel,
        out_shape=(
            jax.ShapeDtypeStruct((rows, 2, 2 * HEAD_SIZE), BF16),
            jax.ShapeDtypeStruct((rows, 2, queries // 2 * HEAD_SIZE), BF16),
        ),
        in_specs=[vmem()] * 9,
        out_specs=(vmem(), vmem()),
        scratch_shapes=[
            pltpu.VMEM((2, group, HEAD_SIZE), F32),
            pltpu.VMEM((rows * queries, HEAD_SIZE), F32),
        ],
        name="merge",
        compiler_params=limit(6),
        cost_estimate=pl.CostEstimate(flops=2_000_000, bytes_accessed=1_000_000, transcendentals=1000),
    )(base, kept, came, cosine, sine, q, top, total, gathered)


def per_device(
    hidden_rows,
    key_value_weight,
    adapter_down_weight,
    adapter_up_weight,
    adapter_ids,
    kv_lengths,
    queries,
    k_cache,
    value_cache,
):
    rows, steps, width = hidden_rows.shape
    owned = adapter_down_weight.shape[0]
    group = rows * steps
    me = lax.axis_index("dp")
    j = lax.axis_index("tensor")
    t, c = j // 2, j % 2

    own = lax.optimization_barrier(hidden_rows.reshape(group, width))
    pair = stack(own, swap_core(own))
    down_other = swap_core(adapter_down_weight)

    k2 = jnp.arange(4, dtype=jnp.int32)[:, None]
    k1 = jnp.arange(4, dtype=jnp.int32)[None, :]
    blocks_of = lambda core: (
        me ^ (16 * core) ^ jnp.where(core == 0, 4 * k1 + k2, 4 * k2 + k1)
    ).reshape(16)
    groups = jnp.concatenate([blocks_of(c), blocks_of(1 - c)])

    start = cross_z(pair)
    low, high = line_halves(start, *[along_x(start, k) for k in (1, 2, 3)])
    low3, high1 = along_y(low, 3), along_y(high, 1)
    q = queries.reshape(rows, -1, HEAD_SIZE)
    top, total, gathered = cached_attention(
        *ready_queries(kv_lengths, q, k_cache.shape[1], start), k_cache, value_cache
    )
    high3, low1 = along_y(high, 3), along_y(low, 1)
    low2, high2 = along_y(low3, 1), along_y(high1, 3)
    blocks = ((low, high), (low1, high1), (low2, high2), (low3, high3))

    codes = make_codes(groups, (me * owned).reshape(1), adapter_ids.reshape(-1, rows), start)
    partial = []
    for k in range(4):
        after = (gathered,) if k == 2 else ()
        partial.append(
            down_block(k, blocks[k], adapter_down_weight, down_other, codes, after)
        )
    partial = jnp.stack(partial)

    chunks = make_chunks(own, low)
    mine = lax.dynamic_index_in_dim(partial, t, 0, keepdims=False).astype(F32)
    came = []
    for m in (1, 2, 3):
        sent = lax.dynamic_index_in_dim(partial, t ^ m, 0, keepdims=False)
        came.append(along_z(jnp.stack([sent, chunks[0][0]]), m))
        mine = mine + came[-1][0].astype(F32)
    both = jnp.stack([mine.astype(BF16), chunks[1][0]])
    slots = [along_z(both, m) for m in (1, 2, 3)]
    wide = widen(adapter_up_weight, both)
    others = swap_core(pack(chunks[0], both, *slots, *came))
    delta = up_blocks(jnp.stack([t, c]), (both, *slots), others, codes, wide)
    full = whole_rows(j.reshape(1), chunks, came, slots, others)

    back = delta[0]
    for k in (1, 3, 2):
        back = back + second_axis(delta[k], k)
    home = back[0]
    for k in (1, 3, 2):
        home = home + first_axis(back[k], k)
    half = full.shape[1] // 2
    base = jnp.dot(full[:, :half], key_value_weight[:half], preferred_element_type=F32)
    kept, sent = small(
        "split",
        split_kernel,
        (jax.ShapeDtypeStruct(home.shape[1:], BF16),) * 2,
        [smem(), vmem(), vmem()],
        (c.reshape(1), home, base),
    )
    came = swap_z(sent)
    base = base + jnp.dot(full[:, half:], key_value_weight[half:], preferred_element_type=F32)

    half = HEAD_SIZE // 2
    frequency = jnp.exp(jnp.arange(half, dtype=F32) * (-2.0 * math.log(500000.0) / HEAD_SIZE))
    positions = (kv_lengths[:, None] + jnp.arange(steps, dtype=jnp.int32)[None, :]).reshape(group)
    angles = positions.astype(F32)[:, None] * frequency
    cosine, sine = jnp.cos(angles), jnp.sin(angles)
    cosine = jnp.concatenate([cosine, cosine], 1)
    sine = jnp.concatenate([-sine, sine], 1)
    return final_merge(base, kept, came, cosine, sine, q, top, total, gathered)


def solution(mesh):
    return jax.shard_map(
        per_device,
        mesh=mesh,
        in_specs=(
            P("dp", None, "tensor"),
            P(None, "tensor"),
            P("dp", "tensor", None),
            P("dp", None, "tensor"),
            P(),
            P("dp"),
            P("dp", None, "tensor"),
            P("dp", None, "tensor"),
            P("dp", None, "tensor"),
        ),
        out_specs=(P("dp", None, "tensor"), P("dp", None, "tensor")),
        check_vma=False,
    )
```

time: 113 us -> 87.3 us (0.77)
  the two profiles are of different devices: /device:TPU:1 before, /device:TPU:32 now
where the time goes in v3:
time: 87.3 us; the launch traced here: 86.6 us
  starting transfers between devices  36.8 us (42%)
  waiting for transfers between devices  29.2 us (33%)
  Pallas kernels  9.12 us (10%)
  local copies, waits for them, and re-layouts  6.04 us (7%)
  matrix products  3.69 us (4%)
  between operations  0.98 us (1%)
    ppermute x6, waiting for transfers between devices, along_z(): lax.ppermute(value, BOTH, pairs_of(lambda z, x, y, t, c: (z, x, y, t ^ k,...  11 us
    ppermute x3, starting transfers between devices, swap_core(): lax.ppermute(value, BOTH, pairs_of(lambda z, x, y, t, c: (z, x, y, t, c ^...  7.68 us
    ppermute x6, starting transfers between devices, along_z(): lax.ppermute(value, BOTH, pairs_of(lambda z, x, y, t, c: (z, x, y, t ^ k,...  7.33 us
    ppermute x6, starting transfers between devices, along_y(): lax.ppermute(value, BOTH, pairs_of(lambda z, x, y, t, c: (z, x ^ (k if c...  6.88 us
    ppermute x6, waiting for transfers between devices, along_y(): lax.ppermute(value, BOTH, pairs_of(lambda z, x, y, t, c: (z, x ^ (k if c...  6.73 us
    ppermute x1, waiting for transfers between devices, swap_z(): lax.ppermute(value, BOTH, pairs_of(lambda z, x, y, t, c: (z ^ 1, x, y, t,...  5.05 us
    ppermute x3, starting transfers between devices, along_x(): lax.ppermute(value, BOTH, pairs_of(lambda z, x, y, t, c: (z, x ^ (0 if c...  4.7 us
    ppermute x3, starting transfers between devices, second_axis(): lax.ppermute(value, BOTH, pairs_of(lambda z, x, y, t, c: (z, x ^ (k if c...  3.73 us
  transfers between devices with their start and end apart: 26, of which 17 were waited for; matrix products, arithmetic and copies ran while one was open for 8% of the time, Pallas kernels for 7%

profile of v3, /device:TPU:32, one launch (start us, length us, event | category | flops | bytes accessed | tf_op | source)
XLA Modules:
  0.0 86.6 jit_solution(12943741404736896575)
XLA Ops:
  3.7 7.5 %collective-permute-start.5 = (bf16[4,1024,128]{2,1,0:T(8,128)(2,1)}, bf16[4,1024,128]{2,1,0:T(8,128)(2,1)S(1)}, u32[]{:S(2)}, u32[]{:S(2)}) collective-permute-start(bf16[4,1024,128]{2,1,0:T(8,128)(2,1)} %own_ref.7), channel_id=1, source_target_pairs={{0,1},{1,0},{2,3},{3,2},{4,5},{5,4},{6,7},{7,6},{8,9},{9,8},{10,11... | collective-permute-start | bytes 3145736 | tf_op jit(solution)/shard_map/ppermute | solution.py:28
  11.2 1.5 %collective-permute-start.2 = (bf16[2,32,1024]{2,1,0:T(8,128)(2,1)S(1)}, bf16[2,32,1024]{2,1,0:T(8,128)(2,1)S(1)}, u32[]{:S(2)}, u32[]{:S(2)}) collective-permute-start(bf16[2,32,1024]{2,1,0:T(8,128)(2,1)S(1)} %collective-permute-done.1.a_ref.after_ref), channel_id=1, source_target_pairs={{0,32},{1,9},{2,34},{3,11},{4,36},{5,13},{6,38},{7,15},{8,40},{9,1... | collective-permute-start | bytes 393224 | tf_op jit(solution)/shard_map/ppermute | solution.py:52
  12.7 2.7 %collective-permute-start.3 = (bf16[2,32,1024]{2,1,0:T(8,128)(2,1)S(1)}, bf16[2,32,1024]{2,1,0:T(8,128)(2,1)}, u32[]{:S(2)}, u32[]{:S(2)}) collective-permute-start(bf16[2,32,1024]{2,1,0:T(8,128)(2,1)S(1)} %collective-permute-done.1.a_ref.after_ref), channel_id=1, source_target_pairs={{0,64},{1,17},{2,66},{3,19},{4,68},{5,21},{6,70},{7,23},{8,72},{9,... | collective-permute-start | bytes 393224 | tf_op jit(solution)/shard_map/ppermute | solution.py:52
  16.1 1.4 %reshape.79.ids_ref = s32[32,16]{1,0:T(8,128)} reshape(s32[512]{0:T(512)} %param.13) | data formatting | bytes 4096 | tf_op jit(solution)/shard_map/reshape | solution.py:413
  22.7 3.1 %collective-permute-start.8 = (bf16[2,2,32,1024]{3,2,1,0:T(8,128)(2,1)S(1)}, bf16[2,2,32,1024]{3,2,1,0:T(8,128)(2,1)S(1)}, u32[]{:S(2)}, u32[]{:S(2)}) collective-permute-start(bf16[2,2,32,1024]{3,2,1,0:T(8,128)(2,1)S(1)} %get-tuple-element.14.after_ref.low_ref), channel_id=1, source_target_pairs={{0,24},{1,97},{2,26},{3,99},{4,28},{5,101},{6,30},{7,103},{8,16},{... | collective-permute-start | bytes 786440 | tf_op jit(solution)/shard_map/ppermute | solution.py:56
  28.7 1.6 %collective-permute-done.8.low_ref = bf16[2,2,32,1024]{3,2,1,0:T(8,128)(2,1)S(1)} collective-permute-done((bf16[2,2,32,1024]{3,2,1,0:T(8,128)(2,1)S(1)}, bf16[2,2,32,1024]{3,2,1,0:T(8,128)(2,1)S(1)}, u32[]{:S(2)}, u32[]{:S(2)}) %collective-permute-start.8) | collective-permute-done | bytes 262176 | tf_op jit(solution)/shard_map/ppermute | solution.py:56
  30.7 1.4 %collective-permute-done.7.high_ref = bf16[2,2,32,1024]{3,2,1,0:T(8,128)(2,1)S(1)} collective-permute-done((bf16[2,2,32,1024]{3,2,1,0:T(8,128)(2,1)S(1)}, bf16[2,2,32,1024]{3,2,1,0:T(8,128)(2,1)S(1)}, u32[]{:S(2)}, u32[]{:S(2)}) %collective-permute-start.7) | collective-permute-done | bytes 262176 | tf_op jit(solution)/shard_map/ppermute | solution.py:56
  36.1 1.7 %collective-permute-done.9.low_ref = bf16[2,2,32,1024]{3,2,1,0:T(8,128)(2,1)S(1)} collective-permute-done((bf16[2,2,32,1024]{3,2,1,0:T(8,128)(2,1)S(1)}, bf16[2,2,32,1024]{3,2,1,0:T(8,128)(2,1)S(1)}, u32[]{:S(2)}, u32[]{:S(2)}) %collective-permute-start.9) | collective-permute-done | bytes 262176 | tf_op jit(solution)/shard_map/ppermute | solution.py:56
  37.8 2.0 %collective-permute-done.10.high_ref = bf16[2,2,32,1024]{3,2,1,0:T(8,128)(2,1)S(1)} collective-permute-done((bf16[2,2,32,1024]{3,2,1,0:T(8,128)(2,1)S(1)}, bf16[2,2,32,1024]{3,2,1,0:T(8,128)(2,1)S(1)}, u32[]{:S(2)}, u32[]{:S(2)}) %collective-permute-start.10) | collective-permute-done | bytes 262176 | tf_op jit(solution)/shard_map/ppermute | solution.py:56
  41.7 1.5 %collective-permute-start.13 = (bf16[2,128,128]{2,1,0:T(8,128)(2,1)S(1)}, bf16[2,128,128]{2,1,0:T(8,128)(2,1)S(1)}, u32[]{:S(2)}, u32[]{:S(2)}) collective-permute-start(bf16[2,128,128]{2,1,0:T(8,128)(2,1)S(1)} %get-tuple-element.33), channel_id=1, source_target_pairs={{0,4},{1,5},{2,6},{3,7},{4,0},{5,1},{6,2},{7,3},{8,12},{9,13},{10,... | collective-permute-start | bytes 196616 | tf_op jit(solution)/shard_map/ppermute | solution.py:60
  44.1 1.3 %collective-permute-done.12.refs_4_.r1 = bf16[2,128,128]{2,1,0:T(8,128)(2,1)S(1)} collective-permute-done((bf16[2,128,128]{2,1,0:T(8,128)(2,1)S(1)}, bf16[2,128,128]{2,1,0:T(8,128)(2,1)S(1)}, u32[]{:S(2)}, u32[]{:S(2)}) %collective-permute-start.12) | collective-permute-done | bytes 65568 | tf_op jit(solution)/shard_map/ppermute | solution.py:60
  45.5 2.4 %collective-permute-done.13.refs_5_.r2 = bf16[2,128,128]{2,1,0:T(8,128)(2,1)S(1)} collective-permute-done((bf16[2,128,128]{2,1,0:T(8,128)(2,1)S(1)}, bf16[2,128,128]{2,1,0:T(8,128)(2,1)S(1)}, u32[]{:S(2)}, u32[]{:S(2)}) %collective-permute-start.13) | collective-permute-done | bytes 65568 | tf_op jit(solution)/shard_map/ppermute | solution.py:60
  47.8 2.2 %collective-permute-done.14.refs_6_.r3 = bf16[2,128,128]{2,1,0:T(8,128)(2,1)S(1)} collective-permute-done((bf16[2,128,128]{2,1,0:T(8,128)(2,1)S(1)}, bf16[2,128,128]{2,1,0:T(8,128)(2,1)S(1)}, u32[]{:S(2)}, u32[]{:S(2)}) %collective-permute-start.14) | collective-permute-done | bytes 65568 | tf_op jit(solution)/shard_map/ppermute | solution.py:60
  51.1 2.0 %collective-permute-start.16 = (bf16[2,128,128]{2,1,0:T(8,128)(2,1)S(1)}, bf16[2,128,128]{2,1,0:T(8,128)(2,1)S(1)}, u32[]{:S(2)}, u32[]{:S(2)}) collective-permute-start(bf16[2,128,128]{2,1,0:T(8,128)(2,1)S(1)} %pad_maximum_fusion.4.refs_0_.after_ref.r0), channel_id=1, source_target_pairs={{0,4},{1,5},{2,6},{3,7},{4,0},{5,1},{6,2},{7,3},{8,12},{9,13},{10,... | collective-permute-start | bytes 196616 | tf_op jit(solution)/shard_map/ppermute | solution.py:60
  53.8 1.3 %collective-permute-done.15.refs_1_.g1.r1 = bf16[2,128,128]{2,1,0:T(8,128)(2,1)S(1)} collective-permute-done((bf16[2,128,128]{2,1,0:T(8,128)(2,1)S(1)}, bf16[2,128,128]{2,1,0:T(8,128)(2,1)S(1)}, u32[]{:S(2)}, u32[]{:S(2)}) %collective-permute-start.15) | collective-permute-done | bytes 65568 | tf_op jit(solution)/shard_map/ppermute | solution.py:60
  55.2 2.1 %collective-permute-done.16.refs_2_.g2.r2 = bf16[2,128,128]{2,1,0:T(8,128)(2,1)S(1)} collective-permute-done((bf16[2,128,128]{2,1,0:T(8,128)(2,1)S(1)}, bf16[2,128,128]{2,1,0:T(8,128)(2,1)S(1)}, u32[]{:S(2)}, u32[]{:S(2)}) %collective-permute-start.16) | collective-permute-done | bytes 65568 | tf_op jit(solution)/shard_map/ppermute | solution.py:60
  57.3 1.6 %collective-permute-done.17.refs_3_.g3.r3 = bf16[2,128,128]{2,1,0:T(8,128)(2,1)S(1)} collective-permute-done((bf16[2,128,128]{2,1,0:T(8,128)(2,1)S(1)}, bf16[2,128,128]{2,1,0:T(8,128)(2,1)S(1)}, u32[]{:S(2)}, u32[]{:S(2)}) %collective-permute-start.17) | collective-permute-done | bytes 65568 | tf_op jit(solution)/shard_map/ppermute | solution.py:60
  60.9 1.5 %up.1 = (bf16[4,2,32,256]{3,2,1,0:T(8,128)(2,1)S(1)}, bf16[4,2,32,256]{3,2,1,0:T(8,128)(2,1)S(1)}, bf16[4,2,32,256]{3,2,1,0:T(8,128)(2,1)S(1)}, bf16[4,2,32,256]{3,2,1,0:T(8,128)(2,1)S(1)}) custom-call(s32[2]{0:T(128)S(1)} %pad_add_fusion.1.t_ref, bf16[2,128,128]{2,1,0:T(8,128)(2,1)S(1)} %pad_maximum_fusion.4.refs_0_.after_ref.r0, ...), custom_call_target="tpu_custom_call" | custom-call | flops 268435456 | bytes 2000000 | tf_op jit(solution)/shard_map/up/pallas_call | solution.py:258
  62.4 2.4 %collective-permute-start.21 = (bf16[4,2,32,256]{3,2,1,0:T(8,128)(2,1)S(1)}, bf16[4,2,32,256]{3,2,1,0:T(8,128)(2,1)S(1)}, u32[]{:S(2)}, u32[]{:S(2)}) collective-permute-start(bf16[4,2,32,256]{3,2,1,0:T(8,128)(2,1)S(1)} %get-tuple-element.23), channel_id=1, source_target_pairs={{0,16},{1,65},{2,18},{3,67},{4,20},{5,69},{6,22},{7,71},{8,24},{9,... | collective-permute-start | bytes 393224 | tf_op jit(solution)/shard_map/ppermute | solution.py:44
  69.0 2.0 %collective-permute-done.20 = bf16[4,2,32,256]{3,2,1,0:T(8,128)(2,1)S(1)} collective-permute-done((bf16[4,2,32,256]{3,2,1,0:T(8,128)(2,1)S(1)}, bf16[4,2,32,256]{3,2,1,0:T(8,128)(2,1)S(1)}, u32[]{:S(2)}, u32[]{:S(2)}) %collective-permute-start.20) | collective-permute-done | bytes 131104 | tf_op jit(solution)/shard_map/ppermute | solution.py:44
  73.2 1.5 %collective-permute-start.22 = (bf16[2,32,256]{2,1,0:T(8,128)(2,1)S(1)}, bf16[2,32,256]{2,1,0:T(8,128)(2,1)S(1)}, u32[]{:S(2)}, u32[]{:S(2)}) collective-permute-start(bf16[2,32,256]{2,1,0:T(8,128)(2,1)S(1)} %get-tuple-element.26), channel_id=1, source_target_pairs={{0,32},{1,9},{2,34},{3,11},{4,36},{5,13},{6,38},{7,15},{8,40},{9,1... | collective-permute-start | bytes 98312 | tf_op jit(solution)/shard_map/ppermute | solution.py:36
  74.7 2.1 %fusion.2.after_ref = f32[32,256]{1,0:T(8,128)S(1)} fusion(bf16[8192,256]{1,0:T(8,128)(2,1)} %param.10, bf16[32,8192]{1,0:T(8,128)(2,1)S(1)} %rows.1), kind=kOutput, calls=%fused_computation.2 | convolution fusion | flops 67108864 | bytes 2392064 | tf_op jit(solution)/shard_map/dot_general | solution.py:443
  77.7 2.2 %collective-permute-start.25 = (bf16[32,256]{1,0:T(8,128)(2,1)S(1)}, bf16[32,256]{1,0:T(8,128)(2,1)S(1)}, u32[]{:S(2)}, u32[]{:S(2)}) collective-permute-start(bf16[32,256]{1,0:T(8,128)(2,1)S(1)} %get-tuple-element.25), channel_id=1, source_target_pairs={{0,128},{1,129},{2,130},{3,131},{4,132},{5,133},{6,134},{7,135},{8... | collective-permute-start | bytes 49160 | tf_op jit(solution)/shard_map/ppermute | solution.py:64
  80.3 5.1 %collective-permute-done.25.came_ref = bf16[32,256]{1,0:T(8,128)(2,1)S(1)} collective-permute-done((bf16[32,256]{1,0:T(8,128)(2,1)S(1)}, bf16[32,256]{1,0:T(8,128)(2,1)S(1)}, u32[]{:S(2)}, u32[]{:S(2)}) %collective-permute-start.25) | collective-permute-done | bytes 16416 | tf_op jit(solution)/shard_map/ppermute | solution.py:64
  (92 shorter events, 31.5 us)
Async XLA Ops:
  3.0 8.2 %collective-permute-start.1 = (bf16[2,32,1024]{2,1,0:T(8,128)(2,1)S(1)}, bf16[2,32,1024]{2,1,0:T(8,128)(2,1)S(1)}, u32[]{:S(2)}, u32[]{:S(2)}) collective-permute-start(bf16[2,32,1024]{2,1,0:T(8,128)(2,1)S(1)} %stack.50), channel_id=1, source_target_pairs={{0,0},{1,129},{2,2},{3,131},{4,4},{5,133},{6,6},{7,135},{8,8},{9,1... | collective-permute-start | bytes 393224 | tf_op jit(solution)/shard_map/ppermute | solution.py:32
  3.7 30.2 %collective-permute-start.5 = (bf16[4,1024,128]{2,1,0:T(8,128)(2,1)}, bf16[4,1024,128]{2,1,0:T(8,128)(2,1)S(1)}, u32[]{:S(2)}, u32[]{:S(2)}) collective-permute-start(bf16[4,1024,128]{2,1,0:T(8,128)(2,1)} %own_ref.7), channel_id=1, source_target_pairs={{0,1},{1,0},{2,3},{3,2},{4,5},{5,4},{6,7},{7,6},{8,9},{9,8},{10,11... | collective-permute-start | bytes 3145736 | tf_op jit(solution)/shard_map/ppermute | solution.py:28
  11.2 10.0 %collective-permute-start.2 = (bf16[2,32,1024]{2,1,0:T(8,128)(2,1)S(1)}, bf16[2,32,1024]{2,1,0:T(8,128)(2,1)S(1)}, u32[]{:S(2)}, u32[]{:S(2)}) collective-permute-start(bf16[2,32,1024]{2,1,0:T(8,128)(2,1)S(1)} %collective-permute-done.1.a_ref.after_ref), channel_id=1, source_target_pairs={{0,32},{1,9},{2,34},{3,11},{4,36},{5,13},{6,38},{7,15},{8,40},{9,1... | collective-permute-start | bytes 393224 | tf_op jit(solution)/shard_map/ppermute | solution.py:52
  12.7 8.5 %collective-permute-start.3 = (bf16[2,32,1024]{2,1,0:T(8,128)(2,1)S(1)}, bf16[2,32,1024]{2,1,0:T(8,128)(2,1)}, u32[]{:S(2)}, u32[]{:S(2)}) collective-permute-start(bf16[2,32,1024]{2,1,0:T(8,128)(2,1)S(1)} %collective-permute-done.1.a_ref.after_ref), channel_id=1, source_target_pairs={{0,64},{1,17},{2,66},{3,19},{4,68},{5,21},{6,70},{7,23},{8,72},{9,... | collective-permute-start | bytes 393224 | tf_op jit(solution)/shard_map/ppermute | solution.py:52
  15.4 6.3 %collective-permute-start.4 = (bf16[2,32,1024]{2,1,0:T(8,128)(2,1)S(1)}, bf16[2,32,1024]{2,1,0:T(8,128)(2,1)}, u32[]{:S(2)}, u32[]{:S(2)}) collective-permute-start(bf16[2,32,1024]{2,1,0:T(8,128)(2,1)S(1)} %collective-permute-done.1.a_ref.after_ref), channel_id=1, source_target_pairs={{0,96},{1,25},{2,98},{3,27},{4,100},{5,29},{6,102},{7,31},{8,104},... | collective-permute-start | bytes 393224 | tf_op jit(solution)/shard_map/ppermute | solution.py:52
  22.7 7.7 %collective-permute-start.8 = (bf16[2,2,32,1024]{3,2,1,0:T(8,128)(2,1)S(1)}, bf16[2,2,32,1024]{3,2,1,0:T(8,128)(2,1)S(1)}, u32[]{:S(2)}, u32[]{:S(2)}) collective-permute-start(bf16[2,2,32,1024]{3,2,1,0:T(8,128)(2,1)S(1)} %get-tuple-element.14.after_ref.low_ref), channel_id=1, source_target_pairs={{0,24},{1,97},{2,26},{3,99},{4,28},{5,101},{6,30},{7,103},{8,16},{... | collective-permute-start | bytes 786440 | tf_op jit(solution)/shard_map/ppermute | solution.py:56
  25.8 6.4 %collective-permute-start.7 = (bf16[2,2,32,1024]{3,2,1,0:T(8,128)(2,1)S(1)}, bf16[2,2,32,1024]{3,2,1,0:T(8,128)(2,1)S(1)}, u32[]{:S(2)}, u32[]{:S(2)}) collective-permute-start(bf16[2,2,32,1024]{3,2,1,0:T(8,128)(2,1)S(1)} %get-tuple-element.17.high_ref), channel_id=1, source_target_pairs={{0,8},{1,33},{2,10},{3,35},{4,12},{5,37},{6,14},{7,39},{8,0},{9,41... | collective-permute-start | bytes 786440 | tf_op jit(solution)/shard_map/ppermute | solution.py:56
  26.7 8.0 %collective-permute-start.11 = (bf16[2,2,32,1024]{3,2,1,0:T(8,128)(2,1)S(1)}, bf16[2,2,32,1024]{3,2,1,0:T(8,128)(2,1)S(1)}, u32[]{:S(2)}, u32[]{:S(2)}) collective-permute-start(bf16[2,2,32,1024]{3,2,1,0:T(8,128)(2,1)S(1)} %get-tuple-element.17.high_ref), channel_id=1, source_target_pairs={{0,24},{1,97},{2,26},{3,99},{4,28},{5,101},{6,30},{7,103},{8,16},{... | collective-permute-start | bytes 786440 | tf_op jit(solution)/shard_map/ppermute | solution.py:56
  27.8 7.6 %collective-permute-start.6 = (bf16[2,2,32,1024]{3,2,1,0:T(8,128)(2,1)S(1)}, bf16[2,2,32,1024]{3,2,1,0:T(8,128)(2,1)S(1)}, u32[]{:S(2)}, u32[]{:S(2)}) collective-permute-start(bf16[2,2,32,1024]{3,2,1,0:T(8,128)(2,1)S(1)} %get-tuple-element.14.after_ref.low_ref), channel_id=1, source_target_pairs={{0,8},{1,33},{2,10},{3,35},{4,12},{5,37},{6,14},{7,39},{8,0},{9,41... | collective-permute-start | bytes 786440 | tf_op jit(solution)/shard_map/ppermute | solution.py:56
  30.4 7.4 %collective-permute-start.9 = (bf16[2,2,32,1024]{3,2,1,0:T(8,128)(2,1)S(1)}, bf16[2,2,32,1024]{3,2,1,0:T(8,128)(2,1)S(1)}, u32[]{:S(2)}, u32[]{:S(2)}) collective-permute-start(bf16[2,2,32,1024]{3,2,1,0:T(8,128)(2,1)S(1)} %collective-permute-done.8.low_ref), channel_id=1, source_target_pairs={{0,8},{1,33},{2,10},{3,35},{4,12},{5,37},{6,14},{7,39},{8,0},{9,41... | collective-permute-start | bytes 786440 | tf_op jit(solution)/shard_map/ppermute | solution.py:56
  32.2 7.6 %collective-permute-start.10 = (bf16[2,2,32,1024]{3,2,1,0:T(8,128)(2,1)S(1)}, bf16[2,2,32,1024]{3,2,1,0:T(8,128)(2,1)S(1)}, u32[]{:S(2)}, u32[]{:S(2)}) collective-permute-start(bf16[2,2,32,1024]{3,2,1,0:T(8,128)(2,1)S(1)} %collective-permute-done.7.high_ref), channel_id=1, source_target_pairs={{0,24},{1,97},{2,26},{3,99},{4,28},{5,101},{6,30},{7,103},{8,16},{... | collective-permute-start | bytes 786440 | tf_op jit(solution)/shard_map/ppermute | solution.py:56
  40.6 4.9 %collective-permute-start.12 = (bf16[2,128,128]{2,1,0:T(8,128)(2,1)S(1)}, bf16[2,128,128]{2,1,0:T(8,128)(2,1)S(1)}, u32[]{:S(2)}, u32[]{:S(2)}) collective-permute-start(bf16[2,128,128]{2,1,0:T(8,128)(2,1)S(1)} %get-tuple-element.34), channel_id=1, source_target_pairs={{0,2},{1,3},{2,0},{3,1},{4,6},{5,7},{6,4},{7,5},{8,10},{9,11},{10,... | collective-permute-start | bytes 196616 | tf_op jit(solution)/shard_map/ppermute | solution.py:60
  41.7 6.2 %collective-permute-start.13 = (bf16[2,128,128]{2,1,0:T(8,128)(2,1)S(1)}, bf16[2,128,128]{2,1,0:T(8,128)(2,1)S(1)}, u32[]{:S(2)}, u32[]{:S(2)}) collective-permute-start(bf16[2,128,128]{2,1,0:T(8,128)(2,1)S(1)} %get-tuple-element.33), channel_id=1, source_target_pairs={{0,4},{1,5},{2,6},{3,7},{4,0},{5,1},{6,2},{7,3},{8,12},{9,13},{10,... | collective-permute-start | bytes 196616 | tf_op jit(solution)/shard_map/ppermute | solution.py:60
  43.1 6.9 %collective-permute-start.14 = (bf16[2,128,128]{2,1,0:T(8,128)(2,1)S(1)}, bf16[2,128,128]{2,1,0:T(8,128)(2,1)S(1)}, u32[]{:S(2)}, u32[]{:S(2)}) collective-permute-start(bf16[2,128,128]{2,1,0:T(8,128)(2,1)S(1)} %get-tuple-element.32), channel_id=1, source_target_pairs={{0,6},{1,7},{2,4},{3,5},{4,2},{5,3},{6,0},{7,1},{8,14},{9,15},{10,... | collective-permute-start | bytes 196616 | tf_op jit(solution)/shard_map/ppermute | solution.py:60
  50.1 5.1 %collective-permute-start.15 = (bf16[2,128,128]{2,1,0:T(8,128)(2,1)S(1)}, bf16[2,128,128]{2,1,0:T(8,128)(2,1)S(1)}, u32[]{:S(2)}, u32[]{:S(2)}) collective-permute-start(bf16[2,128,128]{2,1,0:T(8,128)(2,1)S(1)} %pad_maximum_fusion.4.refs_0_.after_ref.r0), channel_id=1, source_target_pairs={{0,2},{1,3},{2,0},{3,1},{4,6},{5,7},{6,4},{7,5},{8,10},{9,11},{10,... | collective-permute-start | bytes 196616 | tf_op jit(solution)/shard_map/ppermute | solution.py:60
  51.1 6.2 %collective-permute-start.16 = (bf16[2,128,128]{2,1,0:T(8,128)(2,1)S(1)}, bf16[2,128,128]{2,1,0:T(8,128)(2,1)S(1)}, u32[]{:S(2)}, u32[]{:S(2)}) collective-permute-start(bf16[2,128,128]{2,1,0:T(8,128)(2,1)S(1)} %pad_maximum_fusion.4.refs_0_.after_ref.r0), channel_id=1, source_target_pairs={{0,4},{1,5},{2,6},{3,7},{4,0},{5,1},{6,2},{7,3},{8,12},{9,13},{10,... | collective-permute-start | bytes 196616 | tf_op jit(solution)/shard_map/ppermute | solution.py:60
  53.1 5.8 %collective-permute-start.17 = (bf16[2,128,128]{2,1,0:T(8,128)(2,1)S(1)}, bf16[2,128,128]{2,1,0:T(8,128)(2,1)S(1)}, u32[]{:S(2)}, u32[]{:S(2)}) collective-permute-start(bf16[2,128,128]{2,1,0:T(8,128)(2,1)S(1)} %pad_maximum_fusion.4.refs_0_.after_ref.r0), channel_id=1, source_target_pairs={{0,6},{1,7},{2,4},{3,5},{4,2},{5,3},{6,0},{7,1},{8,14},{9,15},{10,... | collective-permute-start | bytes 196616 | tf_op jit(solution)/shard_map/ppermute | solution.py:60
  62.4 6.6 %collective-permute-start.21 = (bf16[4,2,32,256]{3,2,1,0:T(8,128)(2,1)S(1)}, bf16[4,2,32,256]{3,2,1,0:T(8,128)(2,1)S(1)}, u32[]{:S(2)}, u32[]{:S(2)}) collective-permute-start(bf16[4,2,32,256]{3,2,1,0:T(8,128)(2,1)S(1)} %get-tuple-element.23), channel_id=1, source_target_pairs={{0,16},{1,65},{2,18},{3,67},{4,20},{5,69},{6,22},{7,71},{8,24},{9,... | collective-permute-start | bytes 393224 | tf_op jit(solution)/shard_map/ppermute | solution.py:44
  64.8 6.2 %collective-permute-start.20 = (bf16[4,2,32,256]{3,2,1,0:T(8,128)(2,1)S(1)}, bf16[4,2,32,256]{3,2,1,0:T(8,128)(2,1)S(1)}, u32[]{:S(2)}, u32[]{:S(2)}) collective-permute-start(bf16[4,2,32,256]{3,2,1,0:T(8,128)(2,1)S(1)} %get-tuple-element.22), channel_id=1, source_target_pairs={{0,24},{1,97},{2,26},{3,99},{4,28},{5,101},{6,30},{7,103},{8,16},{... | collective-permute-start | bytes 393224 | tf_op jit(solution)/shard_map/ppermute | solution.py:44
  66.1 5.0 %collective-permute-start.19 = (bf16[4,2,32,256]{3,2,1,0:T(8,128)(2,1)S(1)}, bf16[4,2,32,256]{3,2,1,0:T(8,128)(2,1)S(1)}, u32[]{:S(2)}, u32[]{:S(2)}) collective-permute-start(bf16[4,2,32,256]{3,2,1,0:T(8,128)(2,1)S(1)} %get-tuple-element.21), channel_id=1, source_target_pairs={{0,8},{1,33},{2,10},{3,35},{4,12},{5,37},{6,14},{7,39},{8,0},{9,41... | collective-permute-start | bytes 393224 | tf_op jit(solution)/shard_map/ppermute | solution.py:44
  71.1 5.6 %collective-permute-start.24 = (bf16[2,32,256]{2,1,0:T(8,128)(2,1)S(1)}, bf16[2,32,256]{2,1,0:T(8,128)(2,1)S(1)}, u32[]{:S(2)}, u32[]{:S(2)}) collective-permute-start(bf16[2,32,256]{2,1,0:T(8,128)(2,1)S(1)} %get-tuple-element.27), channel_id=1, source_target_pairs={{0,64},{1,17},{2,66},{3,19},{4,68},{5,21},{6,70},{7,23},{8,72},{9,... | collective-permute-start | bytes 98312 | tf_op jit(solution)/shard_map/ppermute | solution.py:36
  72.3 5.1 %collective-permute-start.23 = (bf16[2,32,256]{2,1,0:T(8,128)(2,1)S(1)}, bf16[2,32,256]{2,1,0:T(8,128)(2,1)S(1)}, u32[]{:S(2)}, u32[]{:S(2)}) collective-permute-start(bf16[2,32,256]{2,1,0:T(8,128)(2,1)S(1)} %get-tuple-element.28), channel_id=1, source_target_pairs={{0,96},{1,25},{2,98},{3,27},{4,100},{5,29},{6,102},{7,31},{8,104},... | collective-permute-start | bytes 98312 | tf_op jit(solution)/shard_map/ppermute | solution.py:36
  73.2 4.2 %collective-permute-start.22 = (bf16[2,32,256]{2,1,0:T(8,128)(2,1)S(1)}, bf16[2,32,256]{2,1,0:T(8,128)(2,1)S(1)}, u32[]{:S(2)}, u32[]{:S(2)}) collective-permute-start(bf16[2,32,256]{2,1,0:T(8,128)(2,1)S(1)} %get-tuple-element.26), channel_id=1, source_target_pairs={{0,32},{1,9},{2,34},{3,11},{4,36},{5,13},{6,38},{7,15},{8,40},{9,1... | collective-permute-start | bytes 98312 | tf_op jit(solution)/shard_map/ppermute | solution.py:36
  77.7 7.7 %collective-permute-start.25 = (bf16[32,256]{1,0:T(8,128)(2,1)S(1)}, bf16[32,256]{1,0:T(8,128)(2,1)S(1)}, u32[]{:S(2)}, u32[]{:S(2)}) collective-permute-start(bf16[32,256]{1,0:T(8,128)(2,1)S(1)} %get-tuple-element.25), channel_id=1, source_target_pairs={{0,128},{1,129},{2,130},{3,131},{4,132},{5,133},{6,134},{7,135},{8... | collective-permute-start | bytes 49160 | tf_op jit(solution)/shard_map/ppermute | solution.py:64
  (12 other events, 105.2 us)

commit v4 on v3

--- a/solution.py
+++ b/solution.py
@@ -96,6 +96,25 @@
         compiler_params=limit(mebibytes),
         cost_estimate=pl.CostEstimate(flops=100_000, bytes_accessed=200_000, transcendentals=0),
     )(*args)
+
+
+def flat_kernel(raw_ref, out_ref):
+    out_ref[...] = raw_ref[...].reshape(out_ref.shape)
+
+
+def flat_rows(raw):
+    shape = jax.ShapeDtypeStruct((raw.shape[0] * raw.shape[1], raw.shape[2]), BF16)
+    return small("flat", flat_kernel, shape, [vmem()], (raw,))
+
+
+def rows_kernel(own_ref, other_ref, out_ref):
+    out_ref[0] = own_ref[...]
+    out_ref[1] = other_ref[...].reshape(out_ref.shape[1:])
+
+
+def rows_of(own, other):
+    shape = jax.ShapeDtypeStruct((2, *own.shape), BF16)
+    return small("pair", rows_kernel, shape, [vmem()] * 2, (own, other))
 
 
 def stack_kernel(*refs):
@@ -388,8 +407,8 @@
     j = lax.axis_index("tensor")
     t, c = j // 2, j % 2
 
-    own = lax.optimization_barrier(hidden_rows.reshape(group, width))
-    pair = stack(own, swap_core(own))
+    own = flat_rows(hidden_rows)
+    pair = rows_of(own, swap_core(hidden_rows))
     down_other = swap_core(adapter_down_weight)
 
     k2 = jnp.arange(4, dtype=jnp.int32)[:, None]

time: 87.3 us -> 86.5 us (level)
    reshape x1 -> x0, local copies, waits for them, and re-layouts: 1.02 us -> none  [per_device(): own = lax.optimization_barrier(hidden_rows.reshape(group, width))]
    unnamed x20 -> x22, local copies, waits for them, and re-layouts: 2.31 us -> 3.27 us
where the time goes in v4:
time: 86.5 us; the launch traced here: 85.8 us
  starting transfers between devices  36.8 us (43%)
  waiting for transfers between devices  28.4 us (33%)
  Pallas kernels  9.14 us (11%)
  local copies, waits for them, and re-layouts  5.99 us (7%)
  matrix products  3.69 us (4%)
  between operations  0.99 us (1%)
  other arithmetic  0.87 us (1%)
    ppermute x6, waiting for transfers between devices, along_z(): lax.ppermute(value, BOTH, pairs_of(lambda z, x, y, t, c: (z, x, y, t ^ k,...  11 us
    ppermute x3, starting transfers between devices, swap_core(): lax.ppermute(value, BOTH, pairs_of(lambda z, x, y, t, c: (z, x, y, t, c ^...  7.68 us
    ppermute x6, starting transfers between devices, along_z(): lax.ppermute(value, BOTH, pairs_of(lambda z, x, y, t, c: (z, x, y, t ^ k,...  7.33 us
    ppermute x6, starting transfers between devices, along_y(): lax.ppermute(value, BOTH, pairs_of(lambda z, x, y, t, c: (z, x ^ (k if c...  6.88 us
    ppermute x6, waiting for transfers between devices, along_y(): lax.ppermute(value, BOTH, pairs_of(lambda z, x, y, t, c: (z, x ^ (k if c...  6.73 us
    ppermute x1, waiting for transfers between devices, swap_z(): lax.ppermute(value, BOTH, pairs_of(lambda z, x, y, t, c: (z ^ 1, x, y, t,...  5.05 us
    ppermute x3, starting transfers between devices, along_x(): lax.ppermute(value, BOTH, pairs_of(lambda z, x, y, t, c: (z, x ^ (0 if c...  4.7 us
    ppermute x3, starting transfers between devices, second_axis(): lax.ppermute(value, BOTH, pairs_of(lambda z, x, y, t, c: (z, x ^ (k if c...  3.72 us
  transfers between devices with their start and end apart: 26, of which 17 were waited for; matrix products, arithmetic and copies ran while one was open for 8% of the time, Pallas kernels for 7%

profile of v4, /device:TPU:32, one launch (start us, length us, event | category | flops | bytes accessed | tf_op | source)
XLA Modules:
  0.0 85.8 jit_solution(5165104737703576905)
XLA Ops:
  2.9 7.5 %collective-permute-start.5 = (bf16[4,1024,128]{2,1,0:T(8,128)(2,1)}, bf16[4,1024,128]{2,1,0:T(8,128)(2,1)S(1)}, u32[]{:S(2)}, u32[]{:S(2)}) collective-permute-start(bf16[4,1024,128]{2,1,0:T(8,128)(2,1)} %own_ref.7), channel_id=1, source_target_pairs={{0,1},{1,0},{2,3},{3,2},{4,5},{5,4},{6,7},{7,6},{8,9},{9,8},{10,11... | collective-permute-start | bytes 3145736 | tf_op jit(solution)/shard_map/ppermute | solution.py:28
  10.4 1.5 %collective-permute-start.2 = (bf16[2,32,1024]{2,1,0:T(8,128)(2,1)S(1)}, bf16[2,32,1024]{2,1,0:T(8,128)(2,1)S(1)}, u32[]{:S(2)}, u32[]{:S(2)}) collective-permute-start(bf16[2,32,1024]{2,1,0:T(8,128)(2,1)S(1)} %collective-permute-done.1.a_ref.after_ref), channel_id=1, source_target_pairs={{0,32},{1,9},{2,34},{3,11},{4,36},{5,13},{6,38},{7,15},{8,40},{9,1... | collective-permute-start | bytes 393224 | tf_op jit(solution)/shard_map/ppermute | solution.py:52
  11.9 2.7 %collective-permute-start.3 = (bf16[2,32,1024]{2,1,0:T(8,128)(2,1)S(1)}, bf16[2,32,1024]{2,1,0:T(8,128)(2,1)}, u32[]{:S(2)}, u32[]{:S(2)}) collective-permute-start(bf16[2,32,1024]{2,1,0:T(8,128)(2,1)S(1)} %collective-permute-done.1.a_ref.after_ref), channel_id=1, source_target_pairs={{0,64},{1,17},{2,66},{3,19},{4,68},{5,21},{6,70},{7,23},{8,72},{9,... | collective-permute-start | bytes 393224 | tf_op jit(solution)/shard_map/ppermute | solution.py:52
  15.3 1.4 %reshape.75.ids_ref = s32[32,16]{1,0:T(8,128)} reshape(s32[512]{0:T(512)} %param.13) | data formatting | bytes 4096 | tf_op jit(solution)/shard_map/reshape | solution.py:432
  21.9 3.1 %collective-permute-start.8 = (bf16[2,2,32,1024]{3,2,1,0:T(8,128)(2,1)S(1)}, bf16[2,2,32,1024]{3,2,1,0:T(8,128)(2,1)S(1)}, u32[]{:S(2)}, u32[]{:S(2)}) collective-permute-start(bf16[2,2,32,1024]{3,2,1,0:T(8,128)(2,1)S(1)} %get-tuple-element.14.after_ref.low_ref), channel_id=1, source_target_pairs={{0,24},{1,97},{2,26},{3,99},{4,28},{5,101},{6,30},{7,103},{8,16},{... | collective-permute-start | bytes 786440 | tf_op jit(solution)/shard_map/ppermute | solution.py:56
  27.9 1.6 %collective-permute-done.8.low_ref = bf16[2,2,32,1024]{3,2,1,0:T(8,128)(2,1)S(1)} collective-permute-done((bf16[2,2,32,1024]{3,2,1,0:T(8,128)(2,1)S(1)}, bf16[2,2,32,1024]{3,2,1,0:T(8,128)(2,1)S(1)}, u32[]{:S(2)}, u32[]{:S(2)}) %collective-permute-start.8) | collective-permute-done | bytes 262176 | tf_op jit(solution)/shard_map/ppermute | solution.py:56
  29.9 1.4 %collective-permute-done.7.high_ref = bf16[2,2,32,1024]{3,2,1,0:T(8,128)(2,1)S(1)} collective-permute-done((bf16[2,2,32,1024]{3,2,1,0:T(8,128)(2,1)S(1)}, bf16[2,2,32,1024]{3,2,1,0:T(8,128)(2,1)S(1)}, u32[]{:S(2)}, u32[]{:S(2)}) %collective-permute-start.7) | collective-permute-done | bytes 262176 | tf_op jit(solution)/shard_map/ppermute | solution.py:56
  35.3 1.7 %collective-permute-done.9.low_ref = bf16[2,2,32,1024]{3,2,1,0:T(8,128)(2,1)S(1)} collective-permute-done((bf16[2,2,32,1024]{3,2,1,0:T(8,128)(2,1)S(1)}, bf16[2,2,32,1024]{3,2,1,0:T(8,128)(2,1)S(1)}, u32[]{:S(2)}, u32[]{:S(2)}) %collective-permute-start.9) | collective-permute-done | bytes 262176 | tf_op jit(solution)/shard_map/ppermute | solution.py:56
  37.0 2.0 %collective-permute-done.10.high_ref = bf16[2,2,32,1024]{3,2,1,0:T(8,128)(2,1)S(1)} collective-permute-done((bf16[2,2,32,1024]{3,2,1,0:T(8,128)(2,1)S(1)}, bf16[2,2,32,1024]{3,2,1,0:T(8,128)(2,1)S(1)}, u32[]{:S(2)}, u32[]{:S(2)}) %collective-permute-start.10) | collective-permute-done | bytes 262176 | tf_op jit(solution)/shard_map/ppermute | solution.py:56
  40.9 1.5 %collective-permute-start.13 = (bf16[2,128,128]{2,1,0:T(8,128)(2,1)S(1)}, bf16[2,128,128]{2,1,0:T(8,128)(2,1)S(1)}, u32[]{:S(2)}, u32[]{:S(2)}) collective-permute-start(bf16[2,128,128]{2,1,0:T(8,128)(2,1)S(1)} %get-tuple-element.33), channel_id=1, source_target_pairs={{0,4},{1,5},{2,6},{3,7},{4,0},{5,1},{6,2},{7,3},{8,12},{9,13},{10,... | collective-permute-start | bytes 196616 | tf_op jit(solution)/shard_map/ppermute | solution.py:60
  43.3 1.3 %collective-permute-done.12.refs_4_.r1 = bf16[2,128,128]{2,1,0:T(8,128)(2,1)S(1)} collective-permute-done((bf16[2,128,128]{2,1,0:T(8,128)(2,1)S(1)}, bf16[2,128,128]{2,1,0:T(8,128)(2,1)S(1)}, u32[]{:S(2)}, u32[]{:S(2)}) %collective-permute-start.12) | collective-permute-done | bytes 65568 | tf_op jit(solution)/shard_map/ppermute | solution.py:60
  44.7 2.4 %collective-permute-done.13.refs_5_.r2 = bf16[2,128,128]{2,1,0:T(8,128)(2,1)S(1)} collective-permute-done((bf16[2,128,128]{2,1,0:T(8,128)(2,1)S(1)}, bf16[2,128,128]{2,1,0:T(8,128)(2,1)S(1)}, u32[]{:S(2)}, u32[]{:S(2)}) %collective-permute-start.13) | collective-permute-done | bytes 65568 | tf_op jit(solution)/shard_map/ppermute | solution.py:60
  47.0 2.2 %collective-permute-done.14.refs_6_.r3 = bf16[2,128,128]{2,1,0:T(8,128)(2,1)S(1)} collective-permute-done((bf16[2,128,128]{2,1,0:T(8,128)(2,1)S(1)}, bf16[2,128,128]{2,1,0:T(8,128)(2,1)S(1)}, u32[]{:S(2)}, u32[]{:S(2)}) %collective-permute-start.14) | collective-permute-done | bytes 65568 | tf_op jit(solution)/shard_map/ppermute | solution.py:60
  50.3 2.0 %collective-permute-start.16 = (bf16[2,128,128]{2,1,0:T(8,128)(2,1)S(1)}, bf16[2,128,128]{2,1,0:T(8,128)(2,1)S(1)}, u32[]{:S(2)}, u32[]{:S(2)}) collective-permute-start(bf16[2,128,128]{2,1,0:T(8,128)(2,1)S(1)} %pad_maximum_fusion.4.refs_0_.after_ref.r0), channel_id=1, source_target_pairs={{0,4},{1,5},{2,6},{3,7},{4,0},{5,1},{6,2},{7,3},{8,12},{9,13},{10,... | collective-permute-start | bytes 196616 | tf_op jit(solution)/shard_map/ppermute | solution.py:60
  53.0 1.3 %collective-permute-done.15.refs_1_.g1.r1 = bf16[2,128,128]{2,1,0:T(8,128)(2,1)S(1)} collective-permute-done((bf16[2,128,128]{2,1,0:T(8,128)(2,1)S(1)}, bf16[2,128,128]{2,1,0:T(8,128)(2,1)S(1)}, u32[]{:S(2)}, u32[]{:S(2)}) %collective-permute-start.15) | collective-permute-done | bytes 65568 | tf_op jit(solution)/shard_map/ppermute | solution.py:60
  54.4 2.1 %collective-permute-done.16.refs_2_.g2.r2 = bf16[2,128,128]{2,1,0:T(8,128)(2,1)S(1)} collective-permute-done((bf16[2,128,128]{2,1,0:T(8,128)(2,1)S(1)}, bf16[2,128,128]{2,1,0:T(8,128)(2,1)S(1)}, u32[]{:S(2)}, u32[]{:S(2)}) %collective-permute-start.16) | collective-permute-done | bytes 65568 | tf_op jit(solution)/shard_map/ppermute | solution.py:60
  56.5 1.6 %collective-permute-done.17.refs_3_.g3.r3 = bf16[2,128,128]{2,1,0:T(8,128)(2,1)S(1)} collective-permute-done((bf16[2,128,128]{2,1,0:T(8,128)(2,1)S(1)}, bf16[2,128,128]{2,1,0:T(8,128)(2,1)S(1)}, u32[]{:S(2)}, u32[]{:S(2)}) %collective-permute-start.17) | collective-permute-done | bytes 65568 | tf_op jit(solution)/shard_map/ppermute | solution.py:60
  60.1 1.5 %up.1 = (bf16[4,2,32,256]{3,2,1,0:T(8,128)(2,1)S(1)}, bf16[4,2,32,256]{3,2,1,0:T(8,128)(2,1)S(1)}, bf16[4,2,32,256]{3,2,1,0:T(8,128)(2,1)S(1)}, bf16[4,2,32,256]{3,2,1,0:T(8,128)(2,1)S(1)}) custom-call(s32[2]{0:T(128)S(1)} %pad_add_fusion.1.t_ref, bf16[2,128,128]{2,1,0:T(8,128)(2,1)S(1)} %pad_maximum_fusion.4.refs_0_.after_ref.r0, ...), custom_call_target="tpu_custom_call" | custom-call | flops 268435456 | bytes 2000000 | tf_op jit(solution)/shard_map/up/pallas_call | solution.py:277
  61.6 2.4 %collective-permute-start.21 = (bf16[4,2,32,256]{3,2,1,0:T(8,128)(2,1)S(1)}, bf16[4,2,32,256]{3,2,1,0:T(8,128)(2,1)S(1)}, u32[]{:S(2)}, u32[]{:S(2)}) collective-permute-start(bf16[4,2,32,256]{3,2,1,0:T(8,128)(2,1)S(1)} %get-tuple-element.23), channel_id=1, source_target_pairs={{0,16},{1,65},{2,18},{3,67},{4,20},{5,69},{6,22},{7,71},{8,24},{9,... | collective-permute-start | bytes 393224 | tf_op jit(solution)/shard_map/ppermute | solution.py:44
  68.2 2.0 %collective-permute-done.20 = bf16[4,2,32,256]{3,2,1,0:T(8,128)(2,1)S(1)} collective-permute-done((bf16[4,2,32,256]{3,2,1,0:T(8,128)(2,1)S(1)}, bf16[4,2,32,256]{3,2,1,0:T(8,128)(2,1)S(1)}, u32[]{:S(2)}, u32[]{:S(2)}) %collective-permute-start.20) | collective-permute-done | bytes 131104 | tf_op jit(solution)/shard_map/ppermute | solution.py:44
  72.4 1.5 %collective-permute-start.22 = (bf16[2,32,256]{2,1,0:T(8,128)(2,1)S(1)}, bf16[2,32,256]{2,1,0:T(8,128)(2,1)S(1)}, u32[]{:S(2)}, u32[]{:S(2)}) collective-permute-start(bf16[2,32,256]{2,1,0:T(8,128)(2,1)S(1)} %get-tuple-element.26), channel_id=1, source_target_pairs={{0,32},{1,9},{2,34},{3,11},{4,36},{5,13},{6,38},{7,15},{8,40},{9,1... | collective-permute-start | bytes 98312 | tf_op jit(solution)/shard_map/ppermute | solution.py:36
  73.9 2.1 %fusion.2.after_ref = f32[32,256]{1,0:T(8,128)S(1)} fusion(bf16[8192,256]{1,0:T(8,128)(2,1)} %param.10, bf16[32,8192]{1,0:T(8,128)(2,1)S(1)} %rows.1), kind=kOutput, calls=%fused_computation.2 | convolution fusion | flops 67108864 | bytes 2392064 | tf_op jit(solution)/shard_map/dot_general | solution.py:462
  76.9 2.2 %collective-permute-start.25 = (bf16[32,256]{1,0:T(8,128)(2,1)S(1)}, bf16[32,256]{1,0:T(8,128)(2,1)S(1)}, u32[]{:S(2)}, u32[]{:S(2)}) collective-permute-start(bf16[32,256]{1,0:T(8,128)(2,1)S(1)} %get-tuple-element.25), channel_id=1, source_target_pairs={{0,128},{1,129},{2,130},{3,131},{4,132},{5,133},{6,134},{7,135},{8... | collective-permute-start | bytes 49160 | tf_op jit(solution)/shard_map/ppermute | solution.py:64
  79.5 5.1 %collective-permute-done.25.came_ref = bf16[32,256]{1,0:T(8,128)(2,1)S(1)} collective-permute-done((bf16[32,256]{1,0:T(8,128)(2,1)S(1)}, bf16[32,256]{1,0:T(8,128)(2,1)S(1)}, u32[]{:S(2)}, u32[]{:S(2)}) %collective-permute-start.25) | collective-permute-done | bytes 16416 | tf_op jit(solution)/shard_map/ppermute | solution.py:64
  (94 shorter events, 30.7 us)
Async XLA Ops:
  2.2 8.2 %collective-permute-start.1 = (bf16[2,32,1024]{2,1,0:T(8,128)(2,1)S(1)}, bf16[2,32,1024]{2,1,0:T(8,128)(2,1)S(1)}, u32[]{:S(2)}, u32[]{:S(2)}) collective-permute-start(bf16[2,32,1024]{2,1,0:T(8,128)(2,1)S(1)} %pair.1), channel_id=1, source_target_pairs={{0,0},{1,129},{2,2},{3,131},{4,4},{5,133},{6,6},{7,135},{8,8},{9,1... | collective-permute-start | bytes 393224 | tf_op jit(solution)/shard_map/ppermute | solution.py:32
  2.9 30.2 %collective-permute-start.5 = (bf16[4,1024,128]{2,1,0:T(8,128)(2,1)}, bf16[4,1024,128]{2,1,0:T(8,128)(2,1)S(1)}, u32[]{:S(2)}, u32[]{:S(2)}) collective-permute-start(bf16[4,1024,128]{2,1,0:T(8,128)(2,1)} %own_ref.7), channel_id=1, source_target_pairs={{0,1},{1,0},{2,3},{3,2},{4,5},{5,4},{6,7},{7,6},{8,9},{9,8},{10,11... | collective-permute-start | bytes 3145736 | tf_op jit(solution)/shard_map/ppermute | solution.py:28
  10.4 10.0 %collective-permute-start.2 = (bf16[2,32,1024]{2,1,0:T(8,128)(2,1)S(1)}, bf16[2,32,1024]{2,1,0:T(8,128)(2,1)S(1)}, u32[]{:S(2)}, u32[]{:S(2)}) collective-permute-start(bf16[2,32,1024]{2,1,0:T(8,128)(2,1)S(1)} %collective-permute-done.1.a_ref.after_ref), channel_id=1, source_target_pairs={{0,32},{1,9},{2,34},{3,11},{4,36},{5,13},{6,38},{7,15},{8,40},{9,1... | collective-permute-start | bytes 393224 | tf_op jit(solution)/shard_map/ppermute | solution.py:52
  11.9 8.5 %collective-permute-start.3 = (bf16[2,32,1024]{2,1,0:T(8,128)(2,1)S(1)}, bf16[2,32,1024]{2,1,0:T(8,128)(2,1)}, u32[]{:S(2)}, u32[]{:S(2)}) collective-permute-start(bf16[2,32,1024]{2,1,0:T(8,128)(2,1)S(1)} %collective-permute-done.1.a_ref.after_ref), channel_id=1, source_target_pairs={{0,64},{1,17},{2,66},{3,19},{4,68},{5,21},{6,70},{7,23},{8,72},{9,... | collective-permute-start | bytes 393224 | tf_op jit(solution)/shard_map/ppermute | solution.py:52
  14.6 6.3 %collective-permute-start.4 = (bf16[2,32,1024]{2,1,0:T(8,128)(2,1)S(1)}, bf16[2,32,1024]{2,1,0:T(8,128)(2,1)}, u32[]{:S(2)}, u32[]{:S(2)}) collective-permute-start(bf16[2,32,1024]{2,1,0:T(8,128)(2,1)S(1)} %collective-permute-done.1.a_ref.after_ref), channel_id=1, source_target_pairs={{0,96},{1,25},{2,98},{3,27},{4,100},{5,29},{6,102},{7,31},{8,104},... | collective-permute-start | bytes 393224 | tf_op jit(solution)/shard_map/ppermute | solution.py:52
  21.9 7.7 %collective-permute-start.8 = (bf16[2,2,32,1024]{3,2,1,0:T(8,128)(2,1)S(1)}, bf16[2,2,32,1024]{3,2,1,0:T(8,128)(2,1)S(1)}, u32[]{:S(2)}, u32[]{:S(2)}) collective-permute-start(bf16[2,2,32,1024]{3,2,1,0:T(8,128)(2,1)S(1)} %get-tuple-element.14.after_ref.low_ref), channel_id=1, source_target_pairs={{0,24},{1,97},{2,26},{3,99},{4,28},{5,101},{6,30},{7,103},{8,16},{... | collective-permute-start | bytes 786440 | tf_op jit(solution)/shard_map/ppermute | solution.py:56
  25.0 6.4 %collective-permute-start.7 = (bf16[2,2,32,1024]{3,2,1,0:T(8,128)(2,1)S(1)}, bf16[2,2,32,1024]{3,2,1,0:T(8,128)(2,1)S(1)}, u32[]{:S(2)}, u32[]{:S(2)}) collective-permute-start(bf16[2,2,32,1024]{3,2,1,0:T(8,128)(2,1)S(1)} %get-tuple-element.17.high_ref), channel_id=1, source_target_pairs={{0,8},{1,33},{2,10},{3,35},{4,12},{5,37},{6,14},{7,39},{8,0},{9,41... | collective-permute-start | bytes 786440 | tf_op jit(solution)/shard_map/ppermute | solution.py:56
  25.9 8.0 %collective-permute-start.11 = (bf16[2,2,32,1024]{3,2,1,0:T(8,128)(2,1)S(1)}, bf16[2,2,32,1024]{3,2,1,0:T(8,128)(2,1)S(1)}, u32[]{:S(2)}, u32[]{:S(2)}) collective-permute-start(bf16[2,2,32,1024]{3,2,1,0:T(8,128)(2,1)S(1)} %get-tuple-element.17.high_ref), channel_id=1, source_target_pairs={{0,24},{1,97},{2,26},{3,99},{4,28},{5,101},{6,30},{7,103},{8,16},{... | collective-permute-start | bytes 786440 | tf_op jit(solution)/shard_map/ppermute | solution.py:56
  27.0 7.6 %collective-permute-start.6 = (bf16[2,2,32,1024]{3,2,1,0:T(8,128)(2,1)S(1)}, bf16[2,2,32,1024]{3,2,1,0:T(8,128)(2,1)S(1)}, u32[]{:S(2)}, u32[]{:S(2)}) collective-permute-start(bf16[2,2,32,1024]{3,2,1,0:T(8,128)(2,1)S(1)} %get-tuple-element.14.after_ref.low_ref), channel_id=1, source_target_pairs={{0,8},{1,33},{2,10},{3,35},{4,12},{5,37},{6,14},{7,39},{8,0},{9,41... | collective-permute-start | bytes 786440 | tf_op jit(solution)/shard_map/ppermute | solution.py:56
  29.6 7.4 %collective-permute-start.9 = (bf16[2,2,32,1024]{3,2,1,0:T(8,128)(2,1)S(1)}, bf16[2,2,32,1024]{3,2,1,0:T(8,128)(2,1)S(1)}, u32[]{:S(2)}, u32[]{:S(2)}) collective-permute-start(bf16[2,2,32,1024]{3,2,1,0:T(8,128)(2,1)S(1)} %collective-permute-done.8.low_ref), channel_id=1, source_target_pairs={{0,8},{1,33},{2,10},{3,35},{4,12},{5,37},{6,14},{7,39},{8,0},{9,41... | collective-permute-start | bytes 786440 | tf_op jit(solution)/shard_map/ppermute | solution.py:56
  31.4 7.6 %collective-permute-start.10 = (bf16[2,2,32,1024]{3,2,1,0:T(8,128)(2,1)S(1)}, bf16[2,2,32,1024]{3,2,1,0:T(8,128)(2,1)S(1)}, u32[]{:S(2)}, u32[]{:S(2)}) collective-permute-start(bf16[2,2,32,1024]{3,2,1,0:T(8,128)(2,1)S(1)} %collective-permute-done.7.high_ref), channel_id=1, source_target_pairs={{0,24},{1,97},{2,26},{3,99},{4,28},{5,101},{6,30},{7,103},{8,16},{... | collective-permute-start | bytes 786440 | tf_op jit(solution)/shard_map/ppermute | solution.py:56
  39.8 4.9 %collective-permute-start.12 = (bf16[2,128,128]{2,1,0:T(8,128)(2,1)S(1)}, bf16[2,128,128]{2,1,0:T(8,128)(2,1)S(1)}, u32[]{:S(2)}, u32[]{:S(2)}) collective-permute-start(bf16[2,128,128]{2,1,0:T(8,128)(2,1)S(1)} %get-tuple-element.34), channel_id=1, source_target_pairs={{0,2},{1,3},{2,0},{3,1},{4,6},{5,7},{6,4},{7,5},{8,10},{9,11},{10,... | collective-permute-start | bytes 196616 | tf_op jit(solution)/shard_map/ppermute | solution.py:60
  40.9 6.2 %collective-permute-start.13 = (bf16[2,128,128]{2,1,0:T(8,128)(2,1)S(1)}, bf16[2,128,128]{2,1,0:T(8,128)(2,1)S(1)}, u32[]{:S(2)}, u32[]{:S(2)}) collective-permute-start(bf16[2,128,128]{2,1,0:T(8,128)(2,1)S(1)} %get-tuple-element.33), channel_id=1, source_target_pairs={{0,4},{1,5},{2,6},{3,7},{4,0},{5,1},{6,2},{7,3},{8,12},{9,13},{10,... | collective-permute-start | bytes 196616 | tf_op jit(solution)/shard_map/ppermute | solution.py:60
  42.3 6.9 %collective-permute-start.14 = (bf16[2,128,128]{2,1,0:T(8,128)(2,1)S(1)}, bf16[2,128,128]{2,1,0:T(8,128)(2,1)S(1)}, u32[]{:S(2)}, u32[]{:S(2)}) collective-permute-start(bf16[2,128,128]{2,1,0:T(8,128)(2,1)S(1)} %get-tuple-element.32), channel_id=1, source_target_pairs={{0,6},{1,7},{2,4},{3,5},{4,2},{5,3},{6,0},{7,1},{8,14},{9,15},{10,... | collective-permute-start | bytes 196616 | tf_op jit(solution)/shard_map/ppermute | solution.py:60
  49.3 5.1 %collective-permute-start.15 = (bf16[2,128,128]{2,1,0:T(8,128)(2,1)S(1)}, bf16[2,128,128]{2,1,0:T(8,128)(2,1)S(1)}, u32[]{:S(2)}, u32[]{:S(2)}) collective-permute-start(bf16[2,128,128]{2,1,0:T(8,128)(2,1)S(1)} %pad_maximum_fusion.4.refs_0_.after_ref.r0), channel_id=1, source_target_pairs={{0,2},{1,3},{2,0},{3,1},{4,6},{5,7},{6,4},{7,5},{8,10},{9,11},{10,... | collective-permute-start | bytes 196616 | tf_op jit(solution)/shard_map/ppermute | solution.py:60
  50.3 6.2 %collective-permute-start.16 = (bf16[2,128,128]{2,1,0:T(8,128)(2,1)S(1)}, bf16[2,128,128]{2,1,0:T(8,128)(2,1)S(1)}, u32[]{:S(2)}, u32[]{:S(2)}) collective-permute-start(bf16[2,128,128]{2,1,0:T(8,128)(2,1)S(1)} %pad_maximum_fusion.4.refs_0_.after_ref.r0), channel_id=1, source_target_pairs={{0,4},{1,5},{2,6},{3,7},{4,0},{5,1},{6,2},{7,3},{8,12},{9,13},{10,... | collective-permute-start | bytes 196616 | tf_op jit(solution)/shard_map/ppermute | solution.py:60
  52.3 5.8 %collective-permute-start.17 = (bf16[2,128,128]{2,1,0:T(8,128)(2,1)S(1)}, bf16[2,128,128]{2,1,0:T(8,128)(2,1)S(1)}, u32[]{:S(2)}, u32[]{:S(2)}) collective-permute-start(bf16[2,128,128]{2,1,0:T(8,128)(2,1)S(1)} %pad_maximum_fusion.4.refs_0_.after_ref.r0), channel_id=1, source_target_pairs={{0,6},{1,7},{2,4},{3,5},{4,2},{5,3},{6,0},{7,1},{8,14},{9,15},{10,... | collective-permute-start | bytes 196616 | tf_op jit(solution)/shard_map/ppermute | solution.py:60
  61.6 6.6 %collective-permute-start.21 = (bf16[4,2,32,256]{3,2,1,0:T(8,128)(2,1)S(1)}, bf16[4,2,32,256]{3,2,1,0:T(8,128)(2,1)S(1)}, u32[]{:S(2)}, u32[]{:S(2)}) collective-permute-start(bf16[4,2,32,256]{3,2,1,0:T(8,128)(2,1)S(1)} %get-tuple-element.23), channel_id=1, source_target_pairs={{0,16},{1,65},{2,18},{3,67},{4,20},{5,69},{6,22},{7,71},{8,24},{9,... | collective-permute-start | bytes 393224 | tf_op jit(solution)/shard_map/ppermute | solution.py:44
  64.0 6.2 %collective-permute-start.20 = (bf16[4,2,32,256]{3,2,1,0:T(8,128)(2,1)S(1)}, bf16[4,2,32,256]{3,2,1,0:T(8,128)(2,1)S(1)}, u32[]{:S(2)}, u32[]{:S(2)}) collective-permute-start(bf16[4,2,32,256]{3,2,1,0:T(8,128)(2,1)S(1)} %get-tuple-element.22), channel_id=1, source_target_pairs={{0,24},{1,97},{2,26},{3,99},{4,28},{5,101},{6,30},{7,103},{8,16},{... | collective-permute-start | bytes 393224 | tf_op jit(solution)/shard_map/ppermute | solution.py:44
  65.3 5.0 %collective-permute-start.19 = (bf16[4,2,32,256]{3,2,1,0:T(8,128)(2,1)S(1)}, bf16[4,2,32,256]{3,2,1,0:T(8,128)(2,1)S(1)}, u32[]{:S(2)}, u32[]{:S(2)}) collective-permute-start(bf16[4,2,32,256]{3,2,1,0:T(8,128)(2,1)S(1)} %get-tuple-element.21), channel_id=1, source_target_pairs={{0,8},{1,33},{2,10},{3,35},{4,12},{5,37},{6,14},{7,39},{8,0},{9,41... | collective-permute-start | bytes 393224 | tf_op jit(solution)/shard_map/ppermute | solution.py:44
  70.3 5.6 %collective-permute-start.24 = (bf16[2,32,256]{2,1,0:T(8,128)(2,1)S(1)}, bf16[2,32,256]{2,1,0:T(8,128)(2,1)S(1)}, u32[]{:S(2)}, u32[]{:S(2)}) collective-permute-start(bf16[2,32,256]{2,1,0:T(8,128)(2,1)S(1)} %get-tuple-element.27), channel_id=1, source_target_pairs={{0,64},{1,17},{2,66},{3,19},{4,68},{5,21},{6,70},{7,23},{8,72},{9,... | collective-permute-start | bytes 98312 | tf_op jit(solution)/shard_map/ppermute | solution.py:36
  71.5 5.1 %collective-permute-start.23 = (bf16[2,32,256]{2,1,0:T(8,128)(2,1)S(1)}, bf16[2,32,256]{2,1,0:T(8,128)(2,1)S(1)}, u32[]{:S(2)}, u32[]{:S(2)}) collective-permute-start(bf16[2,32,256]{2,1,0:T(8,128)(2,1)S(1)} %get-tuple-element.28), channel_id=1, source_target_pairs={{0,96},{1,25},{2,98},{3,27},{4,100},{5,29},{6,102},{7,31},{8,104},... | collective-permute-start | bytes 98312 | tf_op jit(solution)/shard_map/ppermute | solution.py:36
  72.4 4.2 %collective-permute-start.22 = (bf16[2,32,256]{2,1,0:T(8,128)(2,1)S(1)}, bf16[2,32,256]{2,1,0:T(8,128)(2,1)S(1)}, u32[]{:S(2)}, u32[]{:S(2)}) collective-permute-start(bf16[2,32,256]{2,1,0:T(8,128)(2,1)S(1)} %get-tuple-element.26), channel_id=1, source_target_pairs={{0,32},{1,9},{2,34},{3,11},{4,36},{5,13},{6,38},{7,15},{8,40},{9,1... | collective-permute-start | bytes 98312 | tf_op jit(solution)/shard_map/ppermute | solution.py:36
  76.9 7.7 %collective-permute-start.25 = (bf16[32,256]{1,0:T(8,128)(2,1)S(1)}, bf16[32,256]{1,0:T(8,128)(2,1)S(1)}, u32[]{:S(2)}, u32[]{:S(2)}) collective-permute-start(bf16[32,256]{1,0:T(8,128)(2,1)S(1)} %get-tuple-element.25), channel_id=1, source_target_pairs={{0,128},{1,129},{2,130},{3,131},{4,132},{5,133},{6,134},{7,135},{8... | collective-permute-start | bytes 49160 | tf_op jit(solution)/shard_map/ppermute | solution.py:64
  (13 other events, 105.6 us)
